TPU v7x, 32 devices: a whole 2x2x4 slice. The times are simulated.
32 devices in a mesh: wide: 8 (over z, y), narrow: 4 (over x, core).
Axes of the slice: x: 2, y: 2, z: 4, core: 2. Of those that a mesh axis runs over, the one named last changes fastest.
Arguments:
- inputs: bfloat16 [32, 128, 64, 128], P(None, 'wide', 'narrow'), may hold values from -6 to 6
- cotangent: bfloat16 [32, 128, 64, 128], P(None, 'wide', 'narrow'), may hold values from -6 to 6
- active_list: int32 [8, 4, 24], P('wide', 'narrow'), may hold values from -1 to 63, as said below
- conv_first: bfloat16 [27, 32, 32], replicated, may hold values from -0.21875 to 0.21875
- conv_second: bfloat16 [27, 32, 32], replicated, may hold values from -0.21875 to 0.21875
- bias_first: float32 [32], replicated, may hold values from -4 to 4
Outputs:
- input_grad: bfloat16 [32, 128, 64, 128], P(None, 'wide', 'narrow')
- first_grad: float32 [27, 32, 32], replicated
- second_grad: float32 [27, 32, 32], replicated
- bias_grad: float32 [32], replicated
Inputs may be any that keep to these rules, and one draw needn't show every extreme that they name: `active_list`: each tile's row lists distinct local block numbers of that tile in ascending order, followed by -1 in the remaining slots; every tile has one or more active blocks, and some tile has 24.
All inputs are finite; a program needn't handle non-finite values.
Results may differ from a plain program's by a relative error of at most 0.0051.
Values may be sent and summed in bfloat16 or wider, within the bound.
A program may use at most 128 MiB of HBM per device.

v0:
```python
import functools
import math

import jax
import jax.numpy as jnp
from jax import lax
from jax.experimental import pallas as pl
from jax.experimental.pallas import tpu as pltpu
from jax.sharding import PartitionSpec as P

BX = 2
BY = 2
LANES = 128
GROUP = 6
WGROUP = 4


def toeplitz(taps, channels):
    kinds = taps.shape[0]
    base = taps.reshape(kinds, 3, 3, 3, channels, channels).transpose(0, 3, 4, 1, 2, 5)
    base = base.reshape(kinds, 3, channels, 3, 3 * channels)
    rows = [
        jnp.pad(base, ((0, 0),) * 4 + ((y * channels, (GROUP - 1 - y) * channels),))
        for y in range(GROUP)
    ]
    full = jnp.stack(rows, axis=2)
    return full.reshape(kinds, 3 * GROUP * channels, 3 * (GROUP + 2) * channels)


def shifted(value, step):
    lane = lax.broadcasted_iota(jnp.int32, value.shape, 1)
    moved = pltpu.roll(value, step % LANES, 1)
    return jnp.where(lane == (0 if step == 1 else LANES - 1), 0.0, moved)


def conv_rows(weights, source, row, col, channels):
    span = (GROUP + 2) * channels
    operand = jnp.concatenate(
        [source[pl.ds(row, span), pl.ds(col + p * LANES, 2 * LANES)] for p in range(3)], axis=0
    )
    out = jnp.dot(weights, operand, preferred_element_type=jnp.float32)
    m = GROUP * channels
    halves = []
    for half in range(2):
        part = out[:, half * LANES : (half + 1) * LANES]
        halves.append(
            shifted(part[:m], 1) + part[m : 2 * m] + shifted(part[2 * m :], -1)
        )
    return halves


def grads_kernel(
    channels, ny, nx,
    in_ref, cot_ref, mask_ref, xlo_ref, xhi_ref, ylo_ref, yhi_ref, w_ref, bias_ref,
    out_ref, grad_ref,
    s_in, s_cot, hid, pre, cot_sh, pre_sh, acc1, acc2, bias_acc,
):
    c = channels
    rows = ny * c
    halo = 2 * LANES
    wide = (nx + 4) * LANES
    for which, own, dst in ((0, in_ref, s_in), (1, cot_ref, s_cot)):
        for y in range(2):
            for src, at in ((ylo_ref, y), (yhi_ref, ny + 2 + y)):
                m = jnp.broadcast_to(mask_ref[at].astype(jnp.bfloat16), (c, wide))
                dst[at * c : (at + 1) * c, :] = src[(which * 2 + y) * c : (which * 2 + y + 1) * c, :] * m

        @pl.loop(0, ny)
        def _(y):
            at = pl.ds(pl.multiple_of((y + 2) * c, c), c)
            frm = pl.ds(pl.multiple_of(y * c, c), c)
            side = pl.ds(pl.multiple_of(which * rows + y * c, c), c)
            m = mask_ref[y + 2].astype(jnp.bfloat16)
            dst[at, halo : halo + nx * LANES] = own[frm, :] * jnp.broadcast_to(
                m[:, halo : halo + nx * LANES], (c, nx * LANES)
            )
            dst[at, :halo] = xlo_ref[side, :] * jnp.broadcast_to(m[:, :halo], (c, halo))
            dst[at, halo + nx * LANES :] = xhi_ref[side, :] * jnp.broadcast_to(
                m[:, halo + nx * LANES :], (c, halo)
            )

    m6 = GROUP * c
    for g in range((ny + 2) // GROUP):

        @pl.loop(0, (nx + 2) // 2)
        def _(pair):
            col = pl.multiple_of(pair * halo, halo)
            pres = conv_rows(w_ref[0], s_in, g * m6, col, c)
            backs = conv_rows(w_ref[1], s_cot, g * m6, col, c)
            for half in range(2):
                v = pres[half] + bias_ref[...]
                s = 0.5 * jnp.tanh(0.5 * v) + 0.5
                at = pl.ds(col + half * LANES, LANES)
                keep = mask_ref[g * GROUP + 1 : (g + 1) * GROUP + 1, :, pl.ds(col + (1 + half) * LANES, LANES)]
                keep = jnp.broadcast_to(keep, (GROUP, c, LANES)).reshape(m6, LANES)
                sk = s * keep
                hid[g * m6 : (g + 1) * m6, at] = (v * sk).astype(jnp.bfloat16)
                pre[g * m6 : (g + 1) * m6, at] = (
                    backs[half] * (sk * (1.0 + v * (1.0 - s)))
                ).astype(jnp.bfloat16)

    starts = list(range(0, ny - GROUP + 1, GROUP))
    if starts[-1] + GROUP < ny:
        starts.append(ny - GROUP)
    for y0 in starts:

        @pl.loop(0, nx // 2)
        def _(pair):
            col = pl.multiple_of(pair * halo, halo)
            outs = conv_rows(w_ref[2], pre, y0 * c, col, c)
            for half in range(2):
                keep = mask_ref[y0 + 2 : y0 + 2 + GROUP, :, pl.ds(col + (2 + half) * LANES, LANES)]
                keep = jnp.broadcast_to(keep, (GROUP, c, LANES)).reshape(m6, LANES)
                out_ref[y0 * c : y0 * c + m6, pl.ds(col + half * LANES, LANES)] = (
                    outs[half] * keep
                ).astype(jnp.bfloat16)

    bias_acc[...] = jnp.zeros_like(bias_acc)

    @pl.loop(0, nx)
    def _(x):
        here = pl.multiple_of(x * LANES, LANES)
        at = pl.ds(here, LANES)
        d = s_cot[2 * c : 2 * c + rows, pl.ds(here + halo, LANES)].astype(jnp.float32)
        cot_sh[0, :, at] = shifted(d, -1).astype(jnp.bfloat16)
        cot_sh[1, :, at] = shifted(d, 1).astype(jnp.bfloat16)
        p = pre[c : c + rows, pl.ds(here + LANES, LANES)].astype(jnp.float32)
        pre_sh[0, :, at] = shifted(p, -1).astype(jnp.bfloat16)
        pre_sh[1, :, at] = shifted(p, 1).astype(jnp.bfloat16)
        bias_acc[...] += jnp.sum(p.reshape(ny, c, LANES), axis=0)

    acc1[...] = jnp.zeros_like(acc1)
    acc2[...] = jnp.zeros_like(acc2)
    wr = WGROUP * c
    n = nx * LANES

    def weight_part(acc, p, y, sh, mid, mid_row, mid_col, other, other_row, other_col):
        own = pl.ds(pl.multiple_of(y * c, wr), wr)
        lhs = jnp.concatenate(
            [
                sh[0, own, :],
                mid[pl.ds(pl.multiple_of(mid_row + y * c, c), wr), mid_col : mid_col + n],
                sh[1, own, :],
            ],
            axis=0,
        )
        rhs = other[
            pl.ds(pl.multiple_of(other_row + y * c, c), (WGROUP + 2) * c),
            other_col + p * LANES : other_col + p * LANES + n,
        ]
        acc[p] += lax.dot_general(
            lhs, rhs, (((1,), (1,)), ((), ())), preferred_element_type=jnp.float32
        )

    @pl.loop(0, ny // WGROUP)
    def _(g):
        y = g * WGROUP
        for p in range(3):
            weight_part(acc1, p, y, pre_sh, pre, c, LANES, s_in, c, LANES)
            weight_part(acc2, p, y, cot_sh, s_cot, 2 * c, halo, hid, 0, 0)

    grad_ref[...] = jnp.zeros_like(grad_ref)
    for which, acc in ((0, acc1), (1, acc2)):
        for p in range(3):
            for r in range(3):
                total = acc[p, r * wr : r * wr + c, 0 : 3 * c]
                for y in range(1, WGROUP):
                    total += acc[p, r * wr + y * c : r * wr + (y + 1) * c, y * c : (y + 3) * c]
                base = ((which * 3 + p) * 3 + r) * c
                grad_ref[base : base + c, 0 : 3 * c] = total
    bias_col = jnp.sum(bias_acc[...], axis=1, keepdims=True)
    grad_ref[18 * c : 19 * c, :] = jnp.broadcast_to(bias_col, (c, LANES))


def body(inputs, cotangent, active_list, conv_first, conv_second, bias_first):
    c, nx, ny, nz = inputs.shape
    depth_blocks = nz // 8
    listing = active_list.reshape(-1)
    ids = jnp.arange(BX * BY * depth_blocks, dtype=jnp.int32)
    present = jnp.any(listing[:, None] == ids[None, :], axis=0).astype(jnp.bfloat16)
    present = present.reshape(BX, BY, depth_blocks).transpose(1, 0, 2)
    mask = jnp.repeat(jnp.repeat(jnp.repeat(present, 8, 2), 8, 1), 8, 0).reshape(ny, nx * nz)

    own_in = inputs.transpose(2, 0, 1, 3).reshape(ny * c, nx * nz)
    own_cot = cotangent.transpose(2, 0, 1, 3).reshape(ny * c, nx * nz)

    def exchange(axis, tail, head):
        count = lax.axis_size(axis)
        lo = lax.ppermute(tail, axis, [(i, i + 1) for i in range(count - 1)])
        hi = lax.ppermute(head, axis, [(i + 1, i) for i in range(count - 1)])
        return lo, hi

    w = 2 * nz
    columns = lambda cut: jnp.concatenate([cut(own_in), cut(own_cot), cut(mask)], axis=0)
    xlo, xhi = exchange(
        "wide", columns(lambda a: a[:, -w:]), columns(lambda a: a[:, :w])
    )
    n = ny * c

    def rows(first):
        parts = []
        for base, own, per in ((0, own_in, c), (n, own_cot, c), (2 * n, mask, 1)):
            r0 = 0 if first else (ny - 2) * per
            r1 = r0 + 2 * per
            parts.append(
                jnp.concatenate(
                    [xlo[base + r0 : base + r1], own[r0:r1], xhi[base + r0 : base + r1]], axis=1
                )
            )
        return jnp.concatenate(parts, axis=0)

    ylo, yhi = exchange("narrow", rows(False), rows(True))
    mask_mid = jnp.concatenate([xlo[2 * n :], mask, xhi[2 * n :]], axis=1)
    full_mask = jnp.concatenate([ylo[4 * c :], mask_mid, yhi[4 * c :]], axis=0)
    full_mask = full_mask.astype(jnp.float32).reshape(ny + 4, 1, (nx + 4) * nz)

    taps = jnp.stack(
        [
            conv_first,
            conv_second[::-1].transpose(0, 2, 1),
            conv_first[::-1].transpose(0, 2, 1),
        ]
    )
    weights = toeplitz(taps, c)
    bias = jnp.broadcast_to(bias_first[None, :, None], (GROUP, c, LANES)).reshape(-1, LANES)

    vmem = pl.BlockSpec(memory_space=pltpu.VMEM)
    bf = jnp.bfloat16
    out, grads = pl.pallas_call(
        functools.partial(grads_kernel, c, ny, nx),
        out_shape=(
            jax.ShapeDtypeStruct((ny * c, nx * nz), bf),
            jax.ShapeDtypeStruct((19 * c, LANES), jnp.float32),
        ),
        in_specs=[vmem] * 9,
        out_specs=(vmem, vmem),
        scratch_shapes=[
            pltpu.VMEM(((ny + 4) * c, (nx + 4) * nz), bf),
            pltpu.VMEM(((ny + 4) * c, (nx + 4) * nz), bf),
            pltpu.VMEM(((ny + 2) * c, (nx + 2) * nz), bf),
            pltpu.VMEM(((ny + 2) * c, (nx + 2) * nz), bf),
            pltpu.VMEM((2, ny * c, nx * nz), bf),
            pltpu.VMEM((2, ny * c, nx * nz), bf),
            pltpu.VMEM((3, 3 * WGROUP * c, (WGROUP + 2) * c), jnp.float32),
            pltpu.VMEM((3, 3 * WGROUP * c, (WGROUP + 2) * c), jnp.float32),
            pltpu.VMEM((c, LANES), jnp.float32),
        ],
        compiler_params=pltpu.CompilerParams(vmem_limit_bytes=56 * 1024 * 1024),
        name="local_grads",
    )(own_in, own_cot, full_mask, xlo[: 2 * n], xhi[: 2 * n], ylo[: 4 * c], yhi[: 4 * c], weights, bias)

    input_grad = out.reshape(ny, c, nx, nz).transpose(1, 2, 0, 3)
    scale = 1.0 / math.sqrt(nx * lax.axis_size("wide") * ny * lax.axis_size("narrow") * nz)
    grads = lax.psum(grads, ("wide", "narrow")) * scale
    both = grads[: 18 * c, : 3 * c].reshape(2, 3, 3, c, 3, c).transpose(0, 1, 4, 2, 3, 5)
    both = both.reshape(2, 27, c, c)
    return input_grad, both[0], both[1], grads[18 * c :, 0]


def solution(mesh):
    return jax.shard_map(
        body,
        mesh=mesh,
        in_specs=(
            P(None, "wide", "narrow", None),
            P(None, "wide", "narrow", None),
            P("wide", "narrow", None),
            P(),
            P(),
            P(),
        ),
        out_specs=(P(None, "wide", "narrow", None), P(), P(), P()),
        check_vma=False,
    )
```

profile of v0, /device:TPU:1, one launch (start us, length us, event | category | flops | bytes accessed | tf_op | source)
XLA Modules:
  0.0 256.7 jit_solution(8569124066395468631)
XLA Ops:
  7.2 2.1 copy.58
  9.9 1.1 copy-done.1
  11.6 1.9 copy.88
  14.0 1.1 fusion.3
  15.9 1.3 collective-permute-start.1
  18.1 5.4 %collective-permute-start = (bf16[1040,256]{1,0:T(8,128)(2,1)}, bf16[1040,256]{1,0:T(8,128)(2,1)}, u32[]{:S(2)}, u32[]{:S(2)}) collective-permute-start(bf16[1040,256]{1,0:T(8,128)(2,1)} %pad_maximum_fusion), channel_id=1, source_target_pairs={{0,4},{4,8},{8,12},{12,16},{16,20},{20,24},{24,28},{1,5},{5,9},{9,... | collective-permute-start | bytes 1597448 | tf_op jit(solution)/shard_map/ppermute | solution.py:189
  23.5 2.0 fusion.2
  25.5 2.0 fusion.1
  32.7 2.6 %copy.68 = bf16[3,3,6,32,3,256]{5,4,3,2,1,0:T(4,128)(2,1)S(1)} copy(bf16[3,3,6,32,3,256]{5,3,4,1,0,2:T(8,128)(2,1)S(1)} %bitcast_dynamic-update-slice_fusion) | data formatting | bytes 5308416 | tf_op jit(solution)/shard_map/stack | solution.py:26
  35.3 5.3 %reshape.104.w_ref = bf16[3,576,768]{2,1,0:T(8,128)(2,1)} reshape(bf16[3,3,6,32,3,256]{5,4,3,2,1,0:T(4,128)(2,1)S(1)} %copy.68) | data formatting | bytes 5308416 | tf_op jit(solution)/shard_map/reshape | solution.py:27
  42.9 1.4 collective-permute-done
  45.8 1.1 maximum_maximum_fusion.1
  46.9 2.4 collective-permute-start.3
  49.4 3.5 %collective-permute-start.2 = (bf16[130,2560]{1,0:T(8,128)(2,1)S(1)}, bf16[130,2560]{1,0:T(8,128)(2,1)S(1)}, u32[]{:S(2)}, u32[]{:S(2)}) collective-permute-start(bf16[130,2560]{1,0:T(8,128)(2,1)S(1)} %maximum_maximum_fusion), channel_id=1, source_target_pairs={{0,1},{1,2},{2,3},{4,5},{5,6},{6,7},{8,9},{9,10},{10,11},{12,13},{... | collective-permute-start | bytes 1996808 | tf_op jit(solution)/shard_map/ppermute | solution.py:189
  54.3 1.9 slice.190.xlo_ref
  56.2 1.9 slice.191.xhi_ref
  58.1 1.1 collective-permute-done.3
  59.3 1.4 collective-permute-done.2
  64.2 52.9 %local_grads.1 = (bf16[512,2048]{1,0:T(8,128)(2,1)}, f32[608,128]{1,0:T(8,128)}) custom-call(bf16[512,2048]{1,0:T(8,128)(2,1)} %bitcast.77, bf16[512,2048]{1,0:T(8,128)(2,1)} %bitcast.79, f32[20,1,2560]{2,1,0:T(1,128)} %copy.69.mask_ref, bf16[1024,256]{1,0:T(8,128)(2,1)} %slice.190.xlo_ref, bf16[1024,256]{1,0:T(8,128)(2,1)} %slice.191.xhi_ref, ...), custom_call_target="tpu_custom_call" | custom-call | tf_op jit(solution)/shard_map/local_grads/pallas_call | solution.py:229
  117.1 2.2 copy.80
  119.3 3.8 %copy.90 = bf16[16,32,16,128]{3,0,2,1:T(8,128)(2,1)} copy(bf16[16,32,16,128]{3,2,1,0:T(8,128)(2,1)S(1)} %bitcast.80) | data formatting | bytes 4194304 | tf_op jit(solution)/shard_map/reshape | solution.py:252
  123.1 122.1 %all-reduce.8.cloned.1.call-done = f32[608,128]{1,0:T(8,128)} async-done(((f32[608,128]{1,0:T(8,128)}), f32[608,128]{1,0:T(8,128)}) %all-reduce.8.cloned.1.call-update) | async-done | bytes 311312 | tf_op jit(solution)/shard_map/psum | solution.py:254
  247.8 1.0 copy.72
  248.8 1.0 copy.73
  (76 shorter events, 19.8 us)
Async XLA Ops:
  7.2 238.0 %all-reduce.8.cloned.1.call-start = ((), (), s32[]{:S(2)}) async-start(), calls=%async_computation | async-start | bytes 622592 | tf_op jit(solution)/shard_map/psum | solution.py:254
  9.3 1.7 copy-start.1
  9.9 4.0 %copy-start = (bf16[64,8,16,128]{3,1,2,0:T(8,128)(2,1)}, bf16[64,8,16,128]{3,1,2,0:T(8,128)(2,1)S(1)}, u32[]{:S(2)}) copy-start(bf16[64,8,16,128]{3,1,2,0:T(8,128)(2,1)S(1)} %copy.89) | copy-start | bytes 6291460
  11.6 1.9 copy-start.8
  13.9 18.7 %copy-start.5 = (bf16[16,2048]{1,0:T(8,128)(2,1)}, bf16[16,2048]{1,0:T(8,128)(2,1)S(1)}, u32[]{:S(2)}) copy-start(bf16[16,2048]{1,0:T(8,128)(2,1)S(1)} %broadcast_bitcast_fusion) | copy-start | bytes 196612
  15.9 25.5 %collective-permute-start.1 = (bf16[1040,256]{1,0:T(8,128)(2,1)}, bf16[1040,256]{1,0:T(8,128)(2,1)}, u32[]{:S(2)}, u32[]{:S(2)}) collective-permute-start(bf16[1040,256]{1,0:T(8,128)(2,1)} %pad_maximum_fusion.1), channel_id=1, source_target_pairs={{4,0},{8,4},{12,8},{16,12},{20,16},{24,20},{28,24},{5,1},{9,5},{13... | collective-permute-start | bytes 1597448 | tf_op jit(solution)/shard_map/ppermute | solution.py:190
  18.1 26.3 %collective-permute-start = (bf16[1040,256]{1,0:T(8,128)(2,1)}, bf16[1040,256]{1,0:T(8,128)(2,1)}, u32[]{:S(2)}, u32[]{:S(2)}) collective-permute-start(bf16[1040,256]{1,0:T(8,128)(2,1)} %pad_maximum_fusion), channel_id=1, source_target_pairs={{0,4},{4,8},{8,12},{12,16},{16,20},{20,24},{24,28},{1,5},{5,9},{9,... | collective-permute-start | bytes 1597448 | tf_op jit(solution)/shard_map/ppermute | solution.py:189
  25.4 2.2 copy-start.4
  27.5 0.9 copy-start.7
  40.6 8.7 %copy-start.2 = (bf16[64,2048]{1,0:T(8,128)(2,1)S(1)}, bf16[64,2048]{1,0:T(8,128)(2,1)}, u32[]{:S(2)}) copy-start(bf16[64,2048]{1,0:T(8,128)(2,1)} %get-tuple-element.38) | copy-start | bytes 786436
  40.6 8.7 %copy-start.3 = (bf16[64,2048]{1,0:T(8,128)(2,1)S(1)}, bf16[64,2048]{1,0:T(8,128)(2,1)}, u32[]{:S(2)}) copy-start(bf16[64,2048]{1,0:T(8,128)(2,1)} %get-tuple-element.39) | copy-start | bytes 786436
  46.9 12.3 %collective-permute-start.3 = (bf16[130,2560]{1,0:T(8,128)(2,1)S(1)}, bf16[130,2560]{1,0:T(8,128)(2,1)S(1)}, u32[]{:S(2)}, u32[]{:S(2)}) collective-permute-start(bf16[130,2560]{1,0:T(8,128)(2,1)S(1)} %maximum_maximum_fusion.1), channel_id=1, source_target_pairs={{1,0},{2,1},{3,2},{5,4},{6,5},{7,6},{9,8},{10,9},{11,10},{13,12},{... | collective-permute-start | bytes 1996808 | tf_op jit(solution)/shard_map/ppermute | solution.py:190
  49.4 8.7 %copy-start.6 = (bf16[16,2048]{1,0:T(8,128)(2,1)S(1)}, bf16[16,2048]{1,0:T(8,128)(2,1)}, u32[]{:S(2)}) copy-start(bf16[16,2048]{1,0:T(8,128)(2,1)} %copy-done.5) | copy-start | bytes 196612
  49.4 11.2 %collective-permute-start.2 = (bf16[130,2560]{1,0:T(8,128)(2,1)S(1)}, bf16[130,2560]{1,0:T(8,128)(2,1)S(1)}, u32[]{:S(2)}, u32[]{:S(2)}) collective-permute-start(bf16[130,2560]{1,0:T(8,128)(2,1)S(1)} %maximum_maximum_fusion), channel_id=1, source_target_pairs={{0,1},{1,2},{2,3},{4,5},{5,6},{6,7},{8,9},{9,10},{10,11},{12,13},{... | collective-permute-start | bytes 1996808 | tf_op jit(solution)/shard_map/ppermute | solution.py:189
Sparse Core Ops, SparseCore 0:
  117.2 127.8 all-reduce.7
where the time goes:
time: 259 us; the launch traced here: 257 us
  waiting for transfers between devices  126 us (49%)
  Pallas kernels  52.9 us (20%)
  local copies, waits for them, and re-layouts  45.9 us (18%)
  between operations  14.4 us (6%)
  starting transfers between devices  12.6 us (5%)
  other arithmetic  4.81 us (2%)
    psum x1, waiting for transfers between devices, body(): grads = lax.psum(grads, ('wide', 'narrow')) * scale  122 us
    pallas_call x1, Pallas kernels, body(): pl.pallas_call(functools.partial(grads_kernel, c, ny, nx), out_shape=(jax...  52.9 us
    ppermute x2, starting transfers between devices, exchange(): lo = lax.ppermute(tail, axis, [(i, i + 1) for i in range(count - 1)])  8.88 us
    unnamed x26, local copies, waits for them, and re-layouts  7.09 us
    slice x9, local copies, waits for them, and re-layouts, rows(): own[r0:r1]  5.92 us
    reshape x1, local copies, waits for them, and re-layouts, toeplitz(): return full.reshape(kinds, 3 * GROUP * channels, 3 * (GROUP + 2) * channels)  5.27 us
  transfers between devices with their start and end apart: 5, of which 4 were waited for; matrix products, arithmetic and copies ran while one was open for 12% of the time, Pallas kernels for 0%

commit v1 on v0

--- a/solution.py
+++ b/solution.py
@@ -169,7 +169,94 @@
                 base = ((which * 3 + p) * 3 + r) * c
                 grad_ref[base : base + c, 0 : 3 * c] = total
     bias_col = jnp.sum(bias_acc[...], axis=1, keepdims=True)
-    grad_ref[18 * c : 19 * c, :] = jnp.broadcast_to(bias_col, (c, LANES))
+    grad_ref[:c, 3 * c :] = jnp.broadcast_to(bias_col, (c, LANES - 3 * c))
+
+
+def total_kernel(
+    wide, narrow, scale, x_ref, out_ref,
+    part, parts_n, parts_w, block, whole,
+    s1, r1, s2, r2, s3, r3, s4, r4,
+):
+    me_w, me_n = lax.axis_index("wide"), lax.axis_index("narrow")
+
+    def send(src, dst, s, r, w, n):
+        copy = pltpu.make_async_remote_copy(
+            src_ref=src, dst_ref=dst, send_sem=s, recv_sem=r,
+            device_id=(w, n), device_id_type=pl.DeviceIdType.MESH,
+        )
+        copy.start()
+        return copy
+
+    barrier = pltpu.get_barrier_semaphore()
+    peers_n = [lax.rem(me_n + k, narrow) for k in range(1, narrow)]
+    peers_w = [lax.rem(me_w + k, wide) for k in range(1, wide)]
+    for n in peers_n:
+        pl.semaphore_signal(barrier, inc=1, device_id=(me_w, n), device_id_type=pl.DeviceIdType.MESH)
+    for w in peers_w:
+        pl.semaphore_signal(barrier, inc=1, device_id=(w, me_n), device_id_type=pl.DeviceIdType.MESH)
+    pl.semaphore_wait(barrier, len(peers_n) + len(peers_w))
+
+    copies = [
+        send(x_ref.at[n], parts_n.at[k], s1.at[k], r1.at[k], me_w, n)
+        for k, n in enumerate(peers_n)
+    ]
+    for copy in copies:
+        copy.wait()
+    total = x_ref[me_n]
+    for k in range(narrow - 1):
+        total += parts_n[k]
+    part[...] = total
+    copies = [
+        send(part.at[w], parts_w.at[k], s2.at[k], r2.at[k], w, me_n)
+        for k, w in enumerate(peers_w)
+    ]
+    for copy in copies:
+        copy.wait()
+    total = part[me_w]
+    for k in range(wide - 1):
+        total += parts_w[k]
+    block[me_w] = total * scale
+    copies = [
+        send(block.at[me_w], block.at[me_w], s3.at[k], r3.at[k], w, me_n)
+        for k, w in enumerate(peers_w)
+    ]
+    for copy in copies:
+        copy.wait()
+    whole[me_n] = block[...]
+    copies = [
+        send(block, whole.at[me_n], s4.at[k], r4.at[k], me_w, n)
+        for k, n in enumerate(peers_n)
+    ]
+    for copy in copies:
+        copy.wait()
+    out_ref[...] = whole[...]
+
+
+def total(grads, wide, narrow, scale):
+    lanes = grads.shape[-1]
+    rows = grads.shape[0] // (wide * narrow)
+    vmem = pl.BlockSpec(memory_space=pltpu.VMEM)
+    f32 = jnp.float32
+    sems = [
+        pltpu.SemaphoreType.DMA((count - 1,))
+        for count in (narrow, narrow, wide, wide, wide, wide, narrow, narrow)
+    ]
+    out = pl.pallas_call(
+        functools.partial(total_kernel, wide, narrow, scale),
+        out_shape=jax.ShapeDtypeStruct((narrow, wide, rows, lanes), f32),
+        in_specs=[vmem],
+        out_specs=vmem,
+        scratch_shapes=[
+            pltpu.VMEM((wide, rows, lanes), f32),
+            pltpu.VMEM((narrow - 1, wide, rows, lanes), f32),
+            pltpu.VMEM((wide - 1, rows, lanes), f32),
+            pltpu.VMEM((wide, rows, lanes), f32),
+            pltpu.VMEM((narrow, wide, rows, lanes), f32),
+        ] + sems,
+        compiler_params=pltpu.CompilerParams(collective_id=0, has_side_effects=True),
+        name="total",
+    )(grads.reshape(narrow, wide, rows, lanes))
+    return out.reshape(-1, lanes)
 
 
 def body(inputs, cotangent, active_list, conv_first, conv_second, bias_first):
@@ -224,13 +311,16 @@
     weights = toeplitz(taps, c)
     bias = jnp.broadcast_to(bias_first[None, :, None], (GROUP, c, LANES)).reshape(-1, LANES)
 
+    wide, narrow = lax.axis_size("wide"), lax.axis_size("narrow")
+    unit = wide * narrow * 8
+    grad_rows = -(-18 * c // unit) * unit
     vmem = pl.BlockSpec(memory_space=pltpu.VMEM)
     bf = jnp.bfloat16
     out, grads = pl.pallas_call(
         functools.partial(grads_kernel, c, ny, nx),
         out_shape=(
             jax.ShapeDtypeStruct((ny * c, nx * nz), bf),
-            jax.ShapeDtypeStruct((19 * c, LANES), jnp.float32),
+            jax.ShapeDtypeStruct((grad_rows, LANES), jnp.float32),
         ),
         in_specs=[vmem] * 9,
         out_specs=(vmem, vmem),
@@ -250,11 +340,11 @@
     )(own_in, own_cot, full_mask, xlo[: 2 * n], xhi[: 2 * n], ylo[: 4 * c], yhi[: 4 * c], weights, bias)
 
     input_grad = out.reshape(ny, c, nx, nz).transpose(1, 2, 0, 3)
-    scale = 1.0 / math.sqrt(nx * lax.axis_size("wide") * ny * lax.axis_size("narrow") * nz)
-    grads = lax.psum(grads, ("wide", "narrow")) * scale
+    scale = 1.0 / math.sqrt(nx * wide * ny * narrow * nz)
+    grads = total(grads, wide, narrow, scale)
     both = grads[: 18 * c, : 3 * c].reshape(2, 3, 3, c, 3, c).transpose(0, 1, 4, 2, 3, 5)
     both = both.reshape(2, 27, c, c)
-    return input_grad, both[0], both[1], grads[18 * c :, 0]
+    return input_grad, both[0], both[1], grads[:c, 3 * c]
 
 
 def solution(mesh):

time: 259 us -> 149 us (0.58)
  waiting for transfers between devices: 126 us -> 3.9 us
  Pallas kernels: 52.9 us -> 78.6 us
  between operations: 14.4 us -> 1.03 us
    psum x1 -> x0, waiting for transfers between devices: 122 us -> none  [body(): grads = lax.psum(grads, ('wide', 'narrow')) * scale]
    pallas_call x0 -> x1, Pallas kernels: none -> 25.7 us  [total(): pl.pallas_call(functools.partial(total_kernel, wide, narrow, scale), out_...]
    unnamed x26 -> x28, local copies, waits for them, and re-layouts: 7.09 us -> 7.83 us
  transfers between devices with their start and end apart: 5 -> 4, of which waited for: 4 -> 3; matrix products, arithmetic and copies ran while one was open for 12% -> 17% of each run, Pallas kernels for 0% -> 0%
where the time goes in v1:
time: 149 us; the launch traced here: 148 us
  Pallas kernels  78.6 us (53%)
  local copies, waits for them, and re-layouts  47.7 us (32%)
  starting transfers between devices  12.6 us (8%)
  waiting for transfers between devices  3.9 us (3%)
  other arithmetic  3.83 us (3%)
    pallas_call x1, Pallas kernels, body(): pl.pallas_call(functools.partial(grads_kernel, c, ny, nx), out_shape=(jax...  52.9 us
    pallas_call x1, Pallas kernels, total(): pl.pallas_call(functools.partial(total_kernel, wide, narrow, scale), out_...  25.7 us
    ppermute x2, starting transfers between devices, exchange(): lo = lax.ppermute(tail, axis, [(i, i + 1) for i in range(count - 1)])  8.88 us
    unnamed x28, local copies, waits for them, and re-layouts  7.83 us
    slice x9, local copies, waits for them, and re-layouts, rows(): own[r0:r1]  5.92 us
    reshape x1, local copies, waits for them, and re-layouts, toeplitz(): return full.reshape(kinds, 3 * GROUP * channels, 3 * (GROUP + 2) * channels)  5.28 us
    reshape x1, local copies, waits for them, and re-layouts, body(): input_grad = out.reshape(ny, c, nx, nz).transpose(1, 2, 0, 3)  3.76 us
    ppermute x2, starting transfers between devices, exchange(): hi = lax.ppermute(head, axis, [(i + 1, i) for i in range(count - 1)])  3.68 us
  transfers between devices with their start and end apart: 4, of which 3 were waited for; matrix products, arithmetic and copies ran while one was open for 17% of the time, Pallas kernels for 0%

profile of v1, /device:TPU:1, one launch (start us, length us, event | category | flops | bytes accessed | tf_op | source)
XLA Modules:
  0.0 147.6 jit_solution(10936679168764102859)
XLA Ops:
  0.6 2.1 %copy.60 = bf16[16,32,16,128]{3,2,1,0:T(8,128)(2,1)S(1)} copy(bf16[16,32,16,128]{3,0,2,1:T(8,128)(2,1)} %bitcast.89) | data formatting | bytes 4194304 | tf_op jit(solution)/shard_map/transpose | solution.py:271
  3.3 1.1 copy-done.1
  5.0 1.9 %copy.93 = bf16[64,8,16,128]{3,1,2,0:T(8,128)(2,1)} copy(bf16[64,8,16,128]{3,2,1,0:T(8,128)(2,1)S(1)} %bitcast.85) | data formatting | bytes 4194304
  7.4 1.1 fusion.3
  9.4 1.3 collective-permute-start.1
  11.5 5.4 %collective-permute-start = (bf16[1040,256]{1,0:T(8,128)(2,1)}, bf16[1040,256]{1,0:T(8,128)(2,1)}, u32[]{:S(2)}, u32[]{:S(2)}) collective-permute-start(bf16[1040,256]{1,0:T(8,128)(2,1)} %pad_maximum_fusion), channel_id=1, source_target_pairs={{0,4},{4,8},{8,12},{12,16},{16,20},{20,24},{24,28},{1,5},{5,9},{9,... | collective-permute-start | bytes 1597448 | tf_op jit(solution)/shard_map/ppermute | solution.py:276
  16.9 2.0 %fusion.2 = (bf16[2,32,16,128]{3,0,2,1:T(2,128)(2,1)S(1)}, bf16[2,32,16,128]{3,0,2,1:T(2,128)(2,1)S(1)}) fusion(bf16[16,32,16,128]{3,0,2,1:T(8,128)(2,1)} %bitcast.87), kind=kLoop, calls=%fused_computation.27 | loop fusion | bytes 1048576 | tf_op jit(solution)/shard_map/slice | solution.py:294
  18.9 2.0 %fusion.1 = (bf16[2,32,16,128]{3,0,2,1:T(2,128)(2,1)S(1)}, bf16[2,32,16,128]{3,0,2,1:T(2,128)(2,1)S(1)}) fusion(bf16[16,32,16,128]{3,0,2,1:T(8,128)(2,1)} %bitcast.90), kind=kLoop, calls=%fused_computation.26 | loop fusion | bytes 1048576 | tf_op jit(solution)/shard_map/slice | solution.py:294
  26.2 2.6 %copy.70 = bf16[3,3,6,32,3,256]{5,4,3,2,1,0:T(4,128)(2,1)S(1)} copy(bf16[3,3,6,32,3,256]{5,3,4,1,0,2:T(8,128)(2,1)S(1)} %bitcast_dynamic-update-slice_fusion) | data formatting | bytes 5308416 | tf_op jit(solution)/shard_map/stack | solution.py:26
  28.8 5.3 %reshape.110.w_ref = bf16[3,576,768]{2,1,0:T(8,128)(2,1)} reshape(bf16[3,3,6,32,3,256]{5,4,3,2,1,0:T(4,128)(2,1)S(1)} %copy.70) | data formatting | bytes 5308416 | tf_op jit(solution)/shard_map/reshape | solution.py:27
  36.4 1.4 collective-permute-done
  39.3 1.1 maximum_maximum_fusion.1
  40.4 2.4 %collective-permute-start.3 = (bf16[130,2560]{1,0:T(8,128)(2,1)S(1)}, bf16[130,2560]{1,0:T(8,128)(2,1)S(1)}, u32[]{:S(2)}, u32[]{:S(2)}) collective-permute-start(bf16[130,2560]{1,0:T(8,128)(2,1)S(1)} %maximum_maximum_fusion.1), channel_id=1, source_target_pairs={{1,0},{2,1},{3,2},{5,4},{6,5},{7,6},{9,8},{10,9},{11,10},{13,12},{... | collective-permute-start | bytes 1996808 | tf_op jit(solution)/shard_map/ppermute | solution.py:277
  42.9 3.5 %collective-permute-start.2 = (bf16[130,2560]{1,0:T(8,128)(2,1)S(1)}, bf16[130,2560]{1,0:T(8,128)(2,1)S(1)}, u32[]{:S(2)}, u32[]{:S(2)}) collective-permute-start(bf16[130,2560]{1,0:T(8,128)(2,1)S(1)} %maximum_maximum_fusion), channel_id=1, source_target_pairs={{0,1},{1,2},{2,3},{4,5},{5,6},{6,7},{8,9},{9,10},{10,11},{12,13},{... | collective-permute-start | bytes 1996808 | tf_op jit(solution)/shard_map/ppermute | solution.py:276
  47.7 1.9 %slice.190.xlo_ref = bf16[1024,256]{1,0:T(8,128)(2,1)} slice(bf16[1040,256]{1,0:T(8,128)(2,1)} %collective-permute-done), slice={[0:1024], [0:256]} | slice | bytes 1048576 | tf_op jit(solution)/shard_map/slice | solution.py:340
  49.6 1.9 %slice.191.xhi_ref = bf16[1024,256]{1,0:T(8,128)(2,1)} slice(bf16[1040,256]{1,0:T(8,128)(2,1)} %collective-permute-done.1), slice={[0:1024], [0:256]} | slice | bytes 1048576 | tf_op jit(solution)/shard_map/slice | solution.py:340
  51.6 1.1 collective-permute-done.3
  52.7 1.4 collective-permute-done.2
  57.6 52.9 %local_grads.1 = (bf16[512,2048]{1,0:T(8,128)(2,1)}, f32[768,128]{1,0:T(8,128)}) custom-call(bf16[512,2048]{1,0:T(8,128)(2,1)} %bitcast.80, bf16[512,2048]{1,0:T(8,128)(2,1)} %bitcast.82, f32[20,1,2560]{2,1,0:T(1,128)} %copy.71.mask_ref, bf16[1024,256]{1,0:T(8,128)(2,1)} %slice.190.xlo_ref, bf16[1024,256]{1,0:T(8,128)(2,1)} %slice.191.xhi_ref, ...), custom_call_target="tpu_custom_call" | custom-call | tf_op jit(solution)/shard_map/local_grads/pallas_call | solution.py:319
  110.5 25.7 %total.1 = f32[4,8,24,128]{3,2,1,0:T(8,128)} custom-call(f32[4,8,24,128]{3,2,1,0:T(8,128)} %bitcast.104), custom_call_target="tpu_custom_call" | custom-call | tf_op jit(solution)/shard_map/total/pallas_call | solution.py:244
  138.0 2.2 %copy.85 = bf16[64,8,16,128]{3,2,1,0:T(8,128)(2,1)S(1)} copy(bf16[64,8,16,128]{3,1,2,0:T(8,128)(2,1)} %bitcast.92) | data formatting | bytes 4194304
  140.2 3.8 %copy.95 = bf16[16,32,16,128]{3,0,2,1:T(8,128)(2,1)} copy(bf16[16,32,16,128]{3,2,1,0:T(8,128)(2,1)S(1)} %bitcast.83) | data formatting | bytes 4194304 | tf_op jit(solution)/shard_map/reshape | solution.py:342
  145.1 1.0 copy.74
  146.0 1.0 copy.75
  (74 shorter events, 20.5 us)
Async XLA Ops:
  2.8 1.7 %copy-start.1 = (bf16[32,16,16,128]{3,2,1,0:T(8,128)(2,1)S(1)}, bf16[32,16,16,128]{3,2,1,0:T(8,128)(2,1)}, u32[]{:S(2)}) copy-start(bf16[32,16,16,128]{3,2,1,0:T(8,128)(2,1)} %param.7) | copy-start | bytes 6291460
  3.3 4.0 %copy-start = (bf16[64,8,16,128]{3,1,2,0:T(8,128)(2,1)}, bf16[64,8,16,128]{3,1,2,0:T(8,128)(2,1)S(1)}, u32[]{:S(2)}) copy-start(bf16[64,8,16,128]{3,1,2,0:T(8,128)(2,1)S(1)} %copy.94) | copy-start | bytes 6291460
  5.0 1.9 %copy-start.8 = (s32[1,1,24]{2,1,0:T(1,128)S(1)}, s32[1,1,24]{2,1,0:T(1,128)}, u32[]{:S(2)}) copy-start(s32[1,1,24]{2,1,0:T(1,128)} %param.8) | copy-start | bytes 292
  7.4 18.7 %copy-start.5 = (bf16[16,2048]{1,0:T(8,128)(2,1)}, bf16[16,2048]{1,0:T(8,128)(2,1)S(1)}, u32[]{:S(2)}) copy-start(bf16[16,2048]{1,0:T(8,128)(2,1)S(1)} %broadcast_bitcast_fusion) | copy-start | bytes 196612
  9.4 25.5 %collective-permute-start.1 = (bf16[1040,256]{1,0:T(8,128)(2,1)}, bf16[1040,256]{1,0:T(8,128)(2,1)}, u32[]{:S(2)}, u32[]{:S(2)}) collective-permute-start(bf16[1040,256]{1,0:T(8,128)(2,1)} %pad_maximum_fusion.1), channel_id=1, source_target_pairs={{4,0},{8,4},{12,8},{16,12},{20,16},{24,20},{28,24},{5,1},{9,5},{13... | collective-permute-start | bytes 1597448 | tf_op jit(solution)/shard_map/ppermute | solution.py:277
  11.5 26.3 %collective-permute-start = (bf16[1040,256]{1,0:T(8,128)(2,1)}, bf16[1040,256]{1,0:T(8,128)(2,1)}, u32[]{:S(2)}, u32[]{:S(2)}) collective-permute-start(bf16[1040,256]{1,0:T(8,128)(2,1)} %pad_maximum_fusion), channel_id=1, source_target_pairs={{0,4},{4,8},{8,12},{12,16},{16,20},{20,24},{24,28},{1,5},{5,9},{9,... | collective-permute-start | bytes 1597448 | tf_op jit(solution)/shard_map/ppermute | solution.py:276
  18.9 2.2 %copy-start.4 = (bf16[27,32,32]{2,1,0:T(8,128)(2,1)S(1)}, bf16[27,32,32]{2,1,0:T(8,128)(2,1)}, u32[]{:S(2)}) copy-start(bf16[27,32,32]{2,1,0:T(8,128)(2,1)} %param.9) | copy-start | bytes 165892
  20.9 0.9 copy-start.7
  34.1 8.7 %copy-start.2 = (bf16[64,2048]{1,0:T(8,128)(2,1)S(1)}, bf16[64,2048]{1,0:T(8,128)(2,1)}, u32[]{:S(2)}) copy-start(bf16[64,2048]{1,0:T(8,128)(2,1)} %get-tuple-element.38) | copy-start | bytes 786436
  34.1 8.7 %copy-start.3 = (bf16[64,2048]{1,0:T(8,128)(2,1)S(1)}, bf16[64,2048]{1,0:T(8,128)(2,1)}, u32[]{:S(2)}) copy-start(bf16[64,2048]{1,0:T(8,128)(2,1)} %get-tuple-element.39) | copy-start | bytes 786436
  40.4 12.3 %collective-permute-start.3 = (bf16[130,2560]{1,0:T(8,128)(2,1)S(1)}, bf16[130,2560]{1,0:T(8,128)(2,1)S(1)}, u32[]{:S(2)}, u32[]{:S(2)}) collective-permute-start(bf16[130,2560]{1,0:T(8,128)(2,1)S(1)} %maximum_maximum_fusion.1), channel_id=1, source_target_pairs={{1,0},{2,1},{3,2},{5,4},{6,5},{7,6},{9,8},{10,9},{11,10},{13,12},{... | collective-permute-start | bytes 1996808 | tf_op jit(solution)/shard_map/ppermute | solution.py:277
  42.8 8.7 %copy-start.6 = (bf16[16,2048]{1,0:T(8,128)(2,1)S(1)}, bf16[16,2048]{1,0:T(8,128)(2,1)}, u32[]{:S(2)}) copy-start(bf16[16,2048]{1,0:T(8,128)(2,1)} %copy-done.5) | copy-start | bytes 196612
  42.9 11.2 %collective-permute-start.2 = (bf16[130,2560]{1,0:T(8,128)(2,1)S(1)}, bf16[130,2560]{1,0:T(8,128)(2,1)S(1)}, u32[]{:S(2)}, u32[]{:S(2)}) collective-permute-start(bf16[130,2560]{1,0:T(8,128)(2,1)S(1)} %maximum_maximum_fusion), channel_id=1, source_target_pairs={{0,1},{1,2},{2,3},{4,5},{5,6},{6,7},{8,9},{9,10},{10,11},{12,13},{... | collective-permute-start | bytes 1996808 | tf_op jit(solution)/shard_map/ppermute | solution.py:276

commit v2 on v1

v2 whole, which is shorter than its diff:
```python
import functools
import math

import jax
import jax.numpy as jnp
from jax import lax
from jax.experimental import pallas as pl
from jax.experimental.pallas import tpu as pltpu
from jax.sharding import PartitionSpec as P

BX = 2
BY = 2
LANES = 128
GROUP = 6
WGROUP = 4


def toeplitz(taps, channels):
    kinds = taps.shape[0]
    base = taps.reshape(kinds, 3, 3, 3, channels, channels).transpose(0, 3, 4, 1, 2, 5)
    base = base.reshape(kinds, 3, channels, 3, 3 * channels)
    rows = [
        jnp.pad(base, ((0, 0),) * 4 + ((y * channels, (GROUP - 1 - y) * channels),))
        for y in range(GROUP)
    ]
    full = jnp.stack(rows, axis=2)
    return full.reshape(kinds, 3 * GROUP * channels, 3 * (GROUP + 2) * channels)


def shifted(value, step):
    lane = lax.broadcasted_iota(jnp.int32, value.shape, 1)
    moved = pltpu.roll(value, step % LANES, 1)
    return jnp.where(lane == (0 if step == 1 else LANES - 1), 0.0, moved)


def conv_rows(weights, source, row, col, channels):
    span = (GROUP + 2) * channels
    operand = jnp.concatenate(
        [source[pl.ds(row, span), pl.ds(col + p * LANES, 2 * LANES)] for p in range(3)], axis=0
    )
    out = jnp.dot(weights, operand, preferred_element_type=jnp.float32)
    m = GROUP * channels
    halves = []
    for half in range(2):
        part = out[:, half * LANES : (half + 1) * LANES]
        halves.append(
            shifted(part[:m], 1) + part[m : 2 * m] + shifted(part[2 * m :], -1)
        )
    return halves


def row_starts(ny):
    starts = list(range(0, ny - GROUP + 1, GROUP))
    if starts[-1] + GROUP < ny:
        starts.append(ny - GROUP)
    return starts


def keep_rows(mask_ref, row, col, channels):
    keep = mask_ref[row : row + GROUP, :, pl.ds(col, LANES)]
    return jnp.broadcast_to(keep, (GROUP, channels, LANES)).reshape(GROUP * channels, LANES)


def grads_kernel(
    channels, ny, nx,
    in_ref, cot_ref, mask_ref, xlo_ref, xhi_ref, ylo_ref, yhi_ref, w_ref, bias_ref,
    pre_ref, grad_ref,
    s_in, s_cot, hid, hid_sh, pre_sh, acc1, acc2, bias_acc,
):
    c = channels
    rows = ny * c
    n = nx * LANES
    wide = n + 2 * LANES
    for which, own, dst in ((0, in_ref, s_in), (1, cot_ref, s_cot)):
        for src, at in ((ylo_ref, 0), (yhi_ref, ny + 1)):
            m = jnp.broadcast_to(mask_ref[at].astype(jnp.bfloat16), (c, wide))
            dst[at * c : (at + 1) * c, :] = src[which * c : (which + 1) * c, :] * m

        @pl.loop(0, ny)
        def _(y):
            at = pl.ds(pl.multiple_of((y + 1) * c, c), c)
            frm = pl.ds(pl.multiple_of(y * c, c), c)
            side = pl.ds(pl.multiple_of(which * rows + y * c, c), c)
            m = mask_ref[y + 1].astype(jnp.bfloat16)
            dst[at, LANES : LANES + n] = own[frm, :] * jnp.broadcast_to(
                m[:, LANES : LANES + n], (c, n)
            )
            dst[at, :LANES] = xlo_ref[side, :] * jnp.broadcast_to(m[:, :LANES], (c, LANES))
            dst[at, LANES + n :] = xhi_ref[side, :] * jnp.broadcast_to(
                m[:, LANES + n :], (c, LANES)
            )

    m6 = GROUP * c
    for y0 in row_starts(ny):

        @pl.loop(0, nx // 2)
        def _(pair):
            col = pl.multiple_of(pair * 2 * LANES, 2 * LANES)
            pres = conv_rows(w_ref[0], s_in, y0 * c, col, c)
            backs = conv_rows(w_ref[1], s_cot, y0 * c, col, c)
            own = slice(y0 * c, y0 * c + m6)
            for half in range(2):
                v = pres[half] + bias_ref[...]
                s = 0.5 * jnp.tanh(0.5 * v) + 0.5
                at = pl.ds(col + half * LANES, LANES)
                keep = keep_rows(mask_ref, y0 + 1, col + (1 + half) * LANES, c)
                sk = s * keep
                h = v * sk
                g = backs[half] * (sk * (1.0 + v * (1.0 - s)))
                hid[own, at] = h.astype(jnp.bfloat16)
                pre_ref[own, at] = g.astype(jnp.bfloat16)
                for k, step in ((0, -1), (1, 1)):
                    hid_sh[k, own, at] = shifted(h, step).astype(jnp.bfloat16)
                    pre_sh[k, own, at] = shifted(g, step).astype(jnp.bfloat16)

    bias_acc[...] = jnp.zeros_like(bias_acc)

    @pl.loop(0, nx)
    def _(x):
        p = pre_ref[:, pl.ds(pl.multiple_of(x * LANES, LANES), LANES)].astype(jnp.float32)
        bias_acc[...] += jnp.sum(p.reshape(ny, c, LANES), axis=0)

    acc1[...] = jnp.zeros_like(acc1)
    acc2[...] = jnp.zeros_like(acc2)
    wr = WGROUP * c

    def weight_part(acc, p, y, sh, mid, other):
        own = pl.ds(pl.multiple_of(y * c, wr), wr)
        lhs = jnp.concatenate([sh[0, own, :], mid[own, :], sh[1, own, :]], axis=0)
        rhs = other[
            pl.ds(pl.multiple_of(y * c, wr), (WGROUP + 2) * c), p * LANES : p * LANES + n
        ]
        acc[p] += lax.dot_general(
            lhs, rhs, (((1,), (1,)), ((), ())), preferred_element_type=jnp.float32
        )

    @pl.loop(0, ny // WGROUP)
    def _(g):
        y = g * WGROUP
        for p in range(3):
            weight_part(acc1, p, y, pre_sh, pre_ref, s_in)
            weight_part(acc2, p, y, hid_sh, hid, s_cot)

    grad_ref[...] = jnp.zeros_like(grad_ref)
    for which, acc in ((0, acc1), (1, acc2)):
        for p in range(3):
            for r in range(3):
                total = acc[p, r * wr : r * wr + c, 0 : 3 * c]
                for y in range(1, WGROUP):
                    total += acc[p, r * wr + y * c : r * wr + (y + 1) * c, y * c : (y + 3) * c]
                tap = p * 3 + r if which == 0 else 8 - (p * 3 + r)
                base = (which * 9 + tap) * c
                grad_ref[base : base + c, 0 : 3 * c] = total
    bias_col = jnp.sum(bias_acc[...], axis=1, keepdims=True)
    grad_ref[:c, 3 * c :] = jnp.broadcast_to(bias_col, (c, LANES - 3 * c))


def input_kernel(
    channels, ny, nx, pre_ref, sides_ref, ends_ref, mask_ref, w_ref, out_ref, pre
):
    c = channels
    n = nx * LANES
    rows = ny * c
    pre[:c, :] = ends_ref[0]
    pre[c + rows :, :] = ends_ref[1]
    pre[c : c + rows, :LANES] = sides_ref[0]
    pre[c : c + rows, LANES + n :] = sides_ref[1]
    pre[c : c + rows, LANES : LANES + n] = pre_ref[...]
    m6 = GROUP * c
    for y0 in row_starts(ny):

        @pl.loop(0, nx // 2)
        def _(pair):
            col = pl.multiple_of(pair * 2 * LANES, 2 * LANES)
            outs = conv_rows(w_ref[2], pre, y0 * c, col, c)
            for half in range(2):
                keep = keep_rows(mask_ref, y0 + 1, col + (1 + half) * LANES, c)
                out_ref[y0 * c : y0 * c + m6, pl.ds(col + half * LANES, LANES)] = (
                    outs[half] * keep
                ).astype(jnp.bfloat16)


def total_kernel(
    wide, narrow, scale, channels, x_ref, pre_ref, out_ref, sides_ref, ends_ref,
    part, parts_n, parts_w, block, whole, sides, ends,
    s1, r1, s2, r2, s3, r3, s4, r4, sh, rh,
):
    me_w, me_n = lax.axis_index("wide"), lax.axis_index("narrow")

    def send(src, dst, s, r, w, n):
        copy = pltpu.make_async_remote_copy(
            src_ref=src, dst_ref=dst, send_sem=s, recv_sem=r,
            device_id=(w, n), device_id_type=pl.DeviceIdType.MESH,
        )
        copy.start()
        return copy

    barrier = pltpu.get_barrier_semaphore()
    peers_n = [lax.rem(me_n + k, narrow) for k in range(1, narrow)]
    peers_w = [lax.rem(me_w + k, wide) for k in range(1, wide)]
    for n in peers_n:
        pl.semaphore_signal(barrier, inc=1, device_id=(me_w, n), device_id_type=pl.DeviceIdType.MESH)
    for w in peers_w:
        pl.semaphore_signal(barrier, inc=1, device_id=(w, me_n), device_id_type=pl.DeviceIdType.MESH)
    w_up, w_down = lax.rem(me_w + 1, wide), lax.rem(me_w + wide - 1, wide)
    n_up, n_down = lax.rem(me_n + 1, narrow), lax.rem(me_n + narrow - 1, narrow)
    corners = [(w, n) for w in (w_up, w_down) for n in (n_up, n_down)]
    for corner in corners:
        pl.semaphore_signal(barrier, inc=1, device_id=corner, device_id_type=pl.DeviceIdType.MESH)
    pl.semaphore_wait(barrier, len(peers_n) + len(peers_w) + len(corners))

    copies = [
        send(x_ref.at[n], parts_n.at[k], s1.at[k], r1.at[k], me_w, n)
        for k, n in enumerate(peers_n)
    ]
    c = channels
    rows, n = pre_ref.shape
    first, last = pl.ds(0, LANES), pl.ds(n - LANES, LANES)
    top, bottom = pl.ds(0, c), pl.ds(rows - c, c)
    mid, far = pl.ds(LANES, n), pl.ds(LANES + n, LANES)
    halos = [
        (pre_ref.at[:, last], sides.at[0], w_up, me_n),
        (pre_ref.at[:, first], sides.at[1], w_down, me_n),
        (pre_ref.at[bottom, :], ends.at[0, :, mid], me_w, n_up),
        (pre_ref.at[top, :], ends.at[1, :, mid], me_w, n_down),
        (pre_ref.at[bottom, last], ends.at[0, :, first], w_up, n_up),
        (pre_ref.at[bottom, first], ends.at[0, :, far], w_down, n_up),
        (pre_ref.at[top, last], ends.at[1, :, first], w_up, n_down),
        (pre_ref.at[top, first], ends.at[1, :, far], w_down, n_down),
    ]
    halos = [send(src, dst, sh.at[k], rh.at[k], w, m) for k, (src, dst, w, m) in enumerate(halos)]
    for copy in copies:
        copy.wait()
    total = x_ref[me_n]
    for k in range(narrow - 1):
        total += parts_n[k]
    part[...] = total
    copies = [
        send(part.at[w], parts_w.at[k], s2.at[k], r2.at[k], w, me_n)
        for k, w in enumerate(peers_w)
    ]
    for copy in copies:
        copy.wait()
    total = part[me_w]
    for k in range(wide - 1):
        total += parts_w[k]
    block[me_w] = total * scale
    copies = [
        send(block.at[me_w], block.at[me_w], s3.at[k], r3.at[k], w, me_n)
        for k, w in enumerate(peers_w)
    ]
    for copy in copies:
        copy.wait()
    whole[me_n] = block[...]
    copies = [
        send(block, whole.at[me_n], s4.at[k], r4.at[k], me_w, n)
        for k, n in enumerate(peers_n)
    ]
    for copy in copies:
        copy.wait()
    out_ref[...] = whole[...]
    for copy in halos:
        copy.wait()
    outside = ((me_w == 0), (me_w == wide - 1), (me_n == 0), (me_n == narrow - 1))
    w_lo, w_hi, n_lo, n_hi = [jnp.where(end, 0.0, 1.0).astype(jnp.float32) for end in outside]

    def scaled(value, factor):
        return (value.astype(jnp.float32) * factor).astype(value.dtype)

    sides_ref[0] = scaled(sides[0], w_lo)
    sides_ref[1] = scaled(sides[1], w_hi)
    for k, factor in ((0, n_lo), (1, n_hi)):
        ends_ref[k, :, :LANES] = scaled(ends[k, :, :LANES], factor * w_lo)
        ends_ref[k, :, LANES : LANES + n] = scaled(ends[k, :, LANES : LANES + n], factor)
        ends_ref[k, :, LANES + n :] = scaled(ends[k, :, LANES + n :], factor * w_hi)


def total(grads, pre, channels, wide, narrow, scale):
    lanes = grads.shape[-1]
    rows = grads.shape[0] // (wide * narrow)
    vmem = pl.BlockSpec(memory_space=pltpu.VMEM)
    f32 = jnp.float32
    sems = [
        pltpu.SemaphoreType.DMA((count - 1,))
        for count in (narrow, narrow, wide, wide, wide, wide, narrow, narrow)
    ]
    side = jax.ShapeDtypeStruct((2, pre.shape[0], LANES), pre.dtype)
    end = jax.ShapeDtypeStruct((2, channels, pre.shape[1] + 2 * LANES), pre.dtype)
    out, sides, ends = pl.pallas_call(
        functools.partial(total_kernel, wide, narrow, scale, channels),
        out_shape=(jax.ShapeDtypeStruct((narrow, wide, rows, lanes), f32), side, end),
        in_specs=[vmem, vmem],
        out_specs=(vmem, vmem, vmem),
        scratch_shapes=[
            pltpu.VMEM((wide, rows, lanes), f32),
            pltpu.VMEM((narrow - 1, wide, rows, lanes), f32),
            pltpu.VMEM((wide - 1, rows, lanes), f32),
            pltpu.VMEM((wide, rows, lanes), f32),
            pltpu.VMEM((narrow, wide, rows, lanes), f32),
            pltpu.VMEM(side.shape, side.dtype),
            pltpu.VMEM(end.shape, end.dtype),
        ] + sems + [pltpu.SemaphoreType.DMA((8,))] * 2,
        compiler_params=pltpu.CompilerParams(
            collective_id=0, has_side_effects=True, vmem_limit_bytes=32 * 1024 * 1024
        ),
        name="total",
    )(grads.reshape(narrow, wide, rows, lanes), pre)
    return out.reshape(-1, lanes), sides, ends


def body(inputs, cotangent, active_list, conv_first, conv_second, bias_first):
    c, nx, ny, nz = inputs.shape
    depth_blocks = nz // 8
    listing = active_list.reshape(-1)
    ids = jnp.arange(BX * BY * depth_blocks, dtype=jnp.int32)
    present = jnp.any(listing[:, None] == ids[None, :], axis=0).astype(jnp.bfloat16)
    present = present.reshape(BX, BY, depth_blocks).transpose(1, 0, 2)
    mask = jnp.repeat(jnp.repeat(jnp.repeat(present, 8, 2), 8, 1), 8, 0).reshape(ny, nx * nz)

    own_in = inputs.transpose(2, 0, 1, 3).reshape(ny * c, nx * nz)
    own_cot = cotangent.transpose(2, 0, 1, 3).reshape(ny * c, nx * nz)

    def exchange(axis, tail, head):
        count = lax.axis_size(axis)
        lo = lax.ppermute(tail, axis, [(i, i + 1) for i in range(count - 1)])
        hi = lax.ppermute(head, axis, [(i + 1, i) for i in range(count - 1)])
        return lo, hi

    columns = lambda cut: jnp.concatenate([cut(own_in), cut(own_cot), cut(mask)], axis=0)
    xlo, xhi = exchange(
        "wide", columns(lambda a: a[:, -nz:]), columns(lambda a: a[:, :nz])
    )
    n = ny * c

    def rows(first):
        parts = []
        for base, own, per in ((0, own_in, c), (n, own_cot, c), (2 * n, mask, 1)):
            r0 = 0 if first else (ny - 1) * per
            r1 = r0 + per
            parts.append(
                jnp.concatenate(
                    [xlo[base + r0 : base + r1], own[r0:r1], xhi[base + r0 : base + r1]], axis=1
                )
            )
        return jnp.concatenate(parts, axis=0)

    ylo, yhi = exchange("narrow", rows(False), rows(True))
    mask_mid = jnp.concatenate([xlo[2 * n :], mask, xhi[2 * n :]], axis=1)
    full_mask = jnp.concatenate([ylo[2 * c :], mask_mid, yhi[2 * c :]], axis=0)
    full_mask = full_mask.astype(jnp.float32).reshape(ny + 2, 1, (nx + 2) * nz)

    taps = jnp.stack(
        [
            conv_first,
            conv_second[::-1].transpose(0, 2, 1),
            conv_first[::-1].transpose(0, 2, 1),
        ]
    )
    weights = toeplitz(taps, c)
    bias = jnp.broadcast_to(bias_first[None, :, None], (GROUP, c, LANES)).reshape(-1, LANES)

    wide, narrow = lax.axis_size("wide"), lax.axis_size("narrow")
    unit = wide * narrow * 8
    grad_rows = -(-18 * c // unit) * unit
    vmem = pl.BlockSpec(memory_space=pltpu.VMEM)
    bf = jnp.bfloat16
    shape = (ny * c, nx * nz)
    halo_shape = ((ny + 2) * c, (nx + 2) * nz)
    acc_shape = (3, 3 * WGROUP * c, (WGROUP + 2) * c)
    params = pltpu.CompilerParams(vmem_limit_bytes=48 * 1024 * 1024)
    pre, grads = pl.pallas_call(
        functools.partial(grads_kernel, c, ny, nx),
        out_shape=(
            jax.ShapeDtypeStruct(shape, bf),
            jax.ShapeDtypeStruct((grad_rows, LANES), jnp.float32),
        ),
        in_specs=[vmem] * 9,
        out_specs=(vmem, vmem),
        scratch_shapes=[
            pltpu.VMEM(halo_shape, bf),
            pltpu.VMEM(halo_shape, bf),
            pltpu.VMEM(shape, bf),
            pltpu.VMEM((2,) + shape, bf),
            pltpu.VMEM((2,) + shape, bf),
            pltpu.VMEM(acc_shape, jnp.float32),
            pltpu.VMEM(acc_shape, jnp.float32),
            pltpu.VMEM((c, LANES), jnp.float32),
        ],
        compiler_params=params,
        name="local_grads",
    )(own_in, own_cot, full_mask, xlo, xhi, ylo, yhi, weights, bias)

    scale = 1.0 / math.sqrt(nx * wide * ny * narrow * nz)
    grads, sides, ends = total(grads, pre, c, wide, narrow, scale)
    out = pl.pallas_call(
        functools.partial(input_kernel, c, ny, nx),
        out_shape=jax.ShapeDtypeStruct(shape, bf),
        in_specs=[vmem] * 5,
        out_specs=vmem,
        scratch_shapes=[pltpu.VMEM(halo_shape, bf)],
        compiler_params=params,
        name="input_grad",
    )(pre, sides, ends, full_mask, weights)
    input_grad = out.reshape(ny, c, nx, nz).transpose(1, 2, 0, 3)
    both = grads[: 18 * c, : 3 * c].reshape(2, 3, 3, c, 3, c)
    first_grad = both[0].transpose(0, 3, 1, 2, 4).reshape(27, c, c)
    second_grad = both[1][:, :, :, ::-1].transpose(0, 3, 1, 4, 2).reshape(27, c, c)
    return input_grad, first_grad, second_grad, grads[:c, 3 * c]


def solution(mesh):
    return jax.shard_map(
        body,
        mesh=mesh,
        in_specs=(
            P(None, "wide", "narrow", None),
            P(None, "wide", "narrow", None),
            P("wide", "narrow", None),
            P(),
            P(),
            P(),
        ),
        out_specs=(P(None, "wide", "narrow", None), P(), P(), P()),
        check_vma=False,
    )
```

time: 149 us -> 140 us (0.940)
  local copies, waits for them, and re-layouts: 47.7 us -> 39.7 us
  waiting for transfers between devices: 3.9 us -> 6.12 us
    pallas_call x1, Pallas kernels: 52.9 us -> 37.6 us  [body(): pl.pallas_call(functools.partial(grads_kernel, c, ny, nx), out_shape=(jax...]
    pallas_call x1 -> x2, Pallas kernels: 25.7 us -> 39.7 us  [the longest x1 25.9 us: total(): pl.pallas_call(functools.partial(total_kernel, wide, narrow, scale, chann...]
    slice x11 -> x4, local copies, waits for them, and re-layouts: 10.7 us -> 1.13 us  [the longest x2 1.04 us: body(): a[:, -nz:]]
    unnamed x28 -> x27, local copies, waits for them, and re-layouts: 7.83 us -> 4.42 us
    ppermute x2, waiting for transfers between devices: 1.13 us -> 4.43 us  [exchange(): hi = lax.ppermute(head, axis, [(i + 1, i) for i in range(count - 1)])]
    reshape x1, local copies, waits for them, and re-layouts: 5.28 us -> 7.97 us  [toeplitz(): return full.reshape(kinds, 3 * GROUP * channels, 3 * (GROUP + 2) * channels)]
    transpose x0 -> x2, local copies, waits for them, and re-layouts: none -> 1.77 us  [the longest x1 0.96 us: body(): both[1][:, :, :, ::-1].transpose(0, 3, 1, 4, 2).reshape(27, c, c)]
    another operation x2, local copies, waits for them, and re-layouts: 2.71 us -> 4.48 us  [toeplitz(): full = jnp.stack(rows, axis=2)]
  transfers between devices with their start and end apart: 4 -> 4, of which waited for: 3 -> 2; matrix products, arithmetic and copies ran while one was open for 17% -> 19% of each run, Pallas kernels for 0% -> 0%
where the time goes in v2:
time: 140 us; the launch traced here: 139 us
  Pallas kernels  77.3 us (55%)
  local copies, waits for them, and re-layouts  39.7 us (28%)
  starting transfers between devices  11.5 us (8%)
  waiting for transfers between devices  6.12 us (4%)
  other arithmetic  3.64 us (3%)
    pallas_call x1, Pallas kernels, body(): pl.pallas_call(functools.partial(grads_kernel, c, ny, nx), out_shape=(jax...  37.6 us
    pallas_call x1, Pallas kernels, total(): pl.pallas_call(functools.partial(total_kernel, wide, narrow, scale, chann...  25.9 us
    pallas_call x1, Pallas kernels, body(): pl.pallas_call(functools.partial(input_kernel, c, ny, nx), out_shape=jax....  13.7 us
    reshape x1, local copies, waits for them, and re-layouts, toeplitz(): return full.reshape(kinds, 3 * GROUP * channels, 3 * (GROUP + 2) * channels)  7.97 us
    ppermute x2, starting transfers between devices, exchange(): lo = lax.ppermute(tail, axis, [(i, i + 1) for i in range(count - 1)])  7.94 us
    slice x5, local copies, waits for them, and re-layouts, rows(): own[r0:r1]  7.44 us
    another operation x2, local copies, waits for them, and re-layouts, toeplitz(): full = jnp.stack(rows, axis=2)  4.48 us
    ppermute x2, waiting for transfers between devices, exchange(): hi = lax.ppermute(head, axis, [(i + 1, i) for i in range(count - 1)])  4.43 us
  transfers between devices with their start and end apart: 4, of which 2 were waited for; matrix products, arithmetic and copies ran while one was open for 19% of the time, Pallas kernels for 0%

profile of v2, /device:TPU:1, one launch (start us, length us, event | category | flops | bytes accessed | tf_op | source)
XLA Modules:
  0.0 139.4 jit_solution(14847707044351461914)
XLA Ops:
  0.6 2.1 %copy.47 = bf16[16,32,16,128]{3,2,1,0:T(8,128)(2,1)S(1)} copy(bf16[16,32,16,128]{3,0,2,1:T(8,128)(2,1)} %bitcast.87) | data formatting | bytes 4194304 | tf_op jit(solution)/shard_map/transpose | solution.py:321
  2.8 1.9 %copy.73 = bf16[64,8,16,128]{3,1,2,0:T(8,128)(2,1)} copy(bf16[64,8,16,128]{3,2,1,0:T(8,128)(2,1)S(1)} %bitcast.83) | data formatting | bytes 4194304
  6.3 1.0 fusion.1
  7.3 0.7 pad_maximum_fusion
  8.0 4.0 %collective-permute-start = (bf16[1040,128]{1,0:T(8,128)(2,1)}, bf16[1040,128]{1,0:T(8,128)(2,1)S(1)}, u32[]{:S(2)}, u32[]{:S(2)}) collective-permute-start(bf16[1040,128]{1,0:T(8,128)(2,1)} %pad_maximum_fusion), channel_id=1, source_target_pairs={{0,4},{4,8},{8,12},{12,16},{16,20},{20,24},{24,28},{1,5},{5,9},{9,... | collective-permute-start | bytes 798728 | tf_op jit(solution)/shard_map/ppermute | solution.py:325
  12.7 1.5 %collective-permute-start.1 = (bf16[1040,128]{1,0:T(8,128)(2,1)}, bf16[1040,128]{1,0:T(8,128)(2,1)S(1)}, u32[]{:S(2)}, u32[]{:S(2)}) collective-permute-start(bf16[1040,128]{1,0:T(8,128)(2,1)} %pad_maximum_fusion.1), channel_id=1, source_target_pairs={{4,0},{8,4},{12,8},{16,12},{20,16},{24,20},{28,24},{5,1},{9,5},{13... | collective-permute-start | bytes 798728 | tf_op jit(solution)/shard_map/ppermute | solution.py:326
  14.2 3.7 %slice_reduce_fusion.3 = (bf16[32,16,128]{2,1,0:T(8,128)(2,1)}, bf16[32,16,128]{2,1,0:T(8,128)(2,1)}) fusion(bf16[16,32,16,128]{3,0,2,1:T(8,128)(2,1)} %bitcast.85), kind=kLoop, calls=%fused_computation.17 | loop fusion | bytes 524288 | tf_op jit(solution)/shard_map/slice | solution.py:342
  17.9 3.6 %slice_reduce_fusion.2 = (bf16[32,16,128]{2,1,0:T(8,128)(2,1)}, bf16[32,16,128]{2,1,0:T(8,128)(2,1)}) fusion(bf16[16,32,16,128]{3,0,2,1:T(8,128)(2,1)} %bitcast.88), kind=kLoop, calls=%fused_computation.16 | loop fusion | bytes 524288 | tf_op jit(solution)/shard_map/slice | solution.py:342
  22.5 1.1 copy.52
  23.8 1.8 %maximum_bitcast_fusion = bf16[3,3,32,3,3,32]{5,4,2,3,1,0:T(4,128)(2,1)} fusion(bf16[1,3,3,3,32,32]{5,2,4,1,3,0:T(4,128)(2,1)S(1)} %copy.52, bf16[1,3,3,3,32,32]{5,2,4,1,3,0:T(4,128)(2,1)S(1)} %copy.51, bf16[1,3,3,3,32,32]{5,2,4,1,3,0:T(4,128)(2,1)S(1)} %copy.50), kind=kLoop, calls=%fused_computation.3 | loop fusion | flops 165888 | bytes 331776 | tf_op jit(solution)/shard_map/transpose | solution.py:20
  25.5 1.6 %reshape.112 = bf16[3,3,32,3,96]{4,2,3,1,0:T(8,128)(2,1)S(1)} reshape(bf16[3,3,32,3,3,32]{5,4,2,3,1,0:T(4,128)(2,1)} %maximum_bitcast_fusion) | data formatting | bytes 331776 | tf_op jit(solution)/shard_map/reshape | solution.py:21
  28.0 4.4 %copy.53 = bf16[3,3,6,32,3,256]{5,4,3,2,1,0:T(4,128)(2,1)} copy(bf16[3,3,6,32,3,256]{5,3,4,1,0,2:T(8,128)(2,1)S(1)} %bitcast_dynamic-update-slice_fusion) | data formatting | bytes 5308416 | tf_op jit(solution)/shard_map/stack | solution.py:26
  32.4 8.0 %reshape.113.w_ref = bf16[3,576,768]{2,1,0:T(8,128)(2,1)} reshape(bf16[3,3,6,32,3,256]{5,4,3,2,1,0:T(4,128)(2,1)} %copy.53) | data formatting | bytes 5308416 | tf_op jit(solution)/shard_map/reshape | solution.py:27
  40.7 4.0 %collective-permute-start.2 = (bf16[65,2304]{1,0:T(8,128)(2,1)S(1)}, bf16[65,2304]{1,0:T(8,128)(2,1)S(1)}, u32[]{:S(2)}, u32[]{:S(2)}) collective-permute-start(bf16[65,2304]{1,0:T(8,128)(2,1)S(1)} %maximum_maximum_fusion), channel_id=1, source_target_pairs={{0,1},{1,2},{2,3},{4,5},{5,6},{6,7},{8,9},{9,10},{10,11},{12,13},{... | collective-permute-start | bytes 898568 | tf_op jit(solution)/shard_map/ppermute | solution.py:325
  44.8 2.1 %collective-permute-start.3 = (bf16[65,2304]{1,0:T(8,128)(2,1)S(1)}, bf16[65,2304]{1,0:T(8,128)(2,1)S(1)}, u32[]{:S(2)}, u32[]{:S(2)}) collective-permute-start(bf16[65,2304]{1,0:T(8,128)(2,1)S(1)} %maximum_maximum_fusion.1), channel_id=1, source_target_pairs={{1,0},{2,1},{3,2},{5,4},{6,5},{7,6},{9,8},{10,9},{11,10},{13,12},{... | collective-permute-start | bytes 898568 | tf_op jit(solution)/shard_map/ppermute | solution.py:326
  47.1 1.7 %collective-permute-done.2.ylo_ref = bf16[65,2304]{1,0:T(8,128)(2,1)S(1)} collective-permute-done((bf16[65,2304]{1,0:T(8,128)(2,1)S(1)}, bf16[65,2304]{1,0:T(8,128)(2,1)S(1)}, u32[]{:S(2)}, u32[]{:S(2)}) %collective-permute-start.2) | collective-permute-done | bytes 299552 | tf_op jit(solution)/shard_map/ppermute | solution.py:325
  48.8 4.4 %collective-permute-done.3.yhi_ref = bf16[65,2304]{1,0:T(8,128)(2,1)S(1)} collective-permute-done((bf16[65,2304]{1,0:T(8,128)(2,1)S(1)}, bf16[65,2304]{1,0:T(8,128)(2,1)S(1)}, u32[]{:S(2)}, u32[]{:S(2)}) %collective-permute-start.3) | collective-permute-done | bytes 299552 | tf_op jit(solution)/shard_map/ppermute | solution.py:326
  53.6 37.6 %local_grads.1 = (bf16[512,2048]{1,0:T(8,128)(2,1)S(1)}, f32[768,128]{1,0:T(8,128)S(1)}) custom-call(bf16[512,2048]{1,0:T(8,128)(2,1)S(1)} %bitcast.75, bf16[512,2048]{1,0:T(8,128)(2,1)} %bitcast.81, f32[18,1,2304]{2,1,0:T(1,128)S(1)} %maximum_convert_fusion.mask_ref, bf16[1040,128]{1,0:T(8,128)(2,1)S(1)} %collective-permute-done.xlo_ref, ...), custom_call_target="tpu_custom_call" | custom-call | tf_op jit(solution)/shard_map/local_grads/pallas_call | solution.py:371
  91.2 25.9 %total.1 = (f32[4,8,24,128]{3,2,1,0:T(8,128)S(1)}, bf16[2,512,128]{2,1,0:T(8,128)(2,1)S(1)}, bf16[2,32,2304]{2,1,0:T(8,128)(2,1)S(1)}) custom-call(f32[4,8,24,128]{3,2,1,0:T(8,128)S(1)} %bitcast.77, bf16[512,2048]{1,0:T(8,128)(2,1)S(1)} %get-tuple-element.9.pre_ref), custom_call_target="tpu_custom_call" | custom-call | tf_op jit(solution)/shard_map/total/pallas_call | solution.py:289
  117.3 13.7 %input_grad.1 = bf16[512,2048]{1,0:T(8,128)(2,1)S(1)} custom-call(bf16[512,2048]{1,0:T(8,128)(2,1)S(1)} %get-tuple-element.9.pre_ref, bf16[2,512,128]{2,1,0:T(8,128)(2,1)S(1)} %get-tuple-element.11.sides_ref, bf16[2,32,2304]{2,1,0:T(8,128)(2,1)S(1)} %get-tuple-element.12.ends_ref, f32[18,1,2304]{2,1,0:T(1,128)S(1)} %maximum_convert_fusion.mask_ref, ...), custom_call_target="tpu_custom_call" | custom-call | tf_op jit(solution)/shard_map/input_grad/pallas_call | solution.py:395
  131.6 3.8 %copy.75 = bf16[16,32,16,128]{3,0,2,1:T(8,128)(2,1)} copy(bf16[16,32,16,128]{3,2,1,0:T(8,128)(2,1)S(1)} %bitcast.82) | data formatting | bytes 4194304 | tf_op jit(solution)/shard_map/reshape | solution.py:404
  135.6 1.1 rev.11
  136.8 1.0 copy.56
  138.0 0.8 copy.55
  (67 shorter events, 6.8 us)
Async XLA Ops:
  2.8 1.9 %copy-start = (bf16[32,16,16,128]{3,2,1,0:T(8,128)(2,1)S(1)}, bf16[32,16,16,128]{3,2,1,0:T(8,128)(2,1)}, u32[]{:S(2)}) copy-start(bf16[32,16,16,128]{3,2,1,0:T(8,128)(2,1)} %param.6) | copy-start | bytes 6291460
  5.2 0.7 copy-start.8
  5.8 15.8 %copy-start.6 = (bf16[27,32,32]{2,1,0:T(8,128)(2,1)S(1)}, bf16[27,32,32]{2,1,0:T(8,128)(2,1)}, u32[]{:S(2)}) copy-start(bf16[27,32,32]{2,1,0:T(8,128)(2,1)} %param.10) | copy-start | bytes 165892
  5.8 16.0 %copy-start.1 = (bf16[27,32,32]{2,1,0:T(8,128)(2,1)S(1)}, bf16[27,32,32]{2,1,0:T(8,128)(2,1)}, u32[]{:S(2)}) copy-start(bf16[27,32,32]{2,1,0:T(8,128)(2,1)} %param.9) | copy-start | bytes 165892
  8.0 32.6 %collective-permute-start = (bf16[1040,128]{1,0:T(8,128)(2,1)}, bf16[1040,128]{1,0:T(8,128)(2,1)S(1)}, u32[]{:S(2)}, u32[]{:S(2)}) collective-permute-start(bf16[1040,128]{1,0:T(8,128)(2,1)} %pad_maximum_fusion), channel_id=1, source_target_pairs={{0,4},{4,8},{8,12},{12,16},{16,20},{20,24},{24,28},{1,5},{5,9},{9,... | collective-permute-start | bytes 798728 | tf_op jit(solution)/shard_map/ppermute | solution.py:325
  12.7 27.9 %collective-permute-start.1 = (bf16[1040,128]{1,0:T(8,128)(2,1)}, bf16[1040,128]{1,0:T(8,128)(2,1)S(1)}, u32[]{:S(2)}, u32[]{:S(2)}) collective-permute-start(bf16[1040,128]{1,0:T(8,128)(2,1)} %pad_maximum_fusion.1), channel_id=1, source_target_pairs={{4,0},{8,4},{12,8},{16,12},{20,16},{24,20},{28,24},{5,1},{9,5},{13... | collective-permute-start | bytes 798728 | tf_op jit(solution)/shard_map/ppermute | solution.py:326
  32.4 8.0 %copy-start.7 = (f32[32]{0:T(128)S(1)}, f32[32]{0:T(128)}, u32[]{:S(2)}) copy-start(f32[32]{0:T(128)} %param.11) | copy-start | bytes 388
  32.4 8.1 %copy-start.4 = (bf16[32,16,128]{2,1,0:T(8,128)(2,1)S(1)}, bf16[32,16,128]{2,1,0:T(8,128)(2,1)}, u32[]{:S(2)}) copy-start(bf16[32,16,128]{2,1,0:T(8,128)(2,1)} %get-tuple-element.14) | copy-start | bytes 393220
  32.4 8.1 %copy-start.5 = (bf16[32,16,128]{2,1,0:T(8,128)(2,1)S(1)}, bf16[32,16,128]{2,1,0:T(8,128)(2,1)}, u32[]{:S(2)}) copy-start(bf16[32,16,128]{2,1,0:T(8,128)(2,1)} %get-tuple-element.16) | copy-start | bytes 393220
  32.4 8.1 %copy-start.2 = (bf16[32,16,128]{2,1,0:T(8,128)(2,1)S(1)}, bf16[32,16,128]{2,1,0:T(8,128)(2,1)}, u32[]{:S(2)}) copy-start(bf16[32,16,128]{2,1,0:T(8,128)(2,1)} %get-tuple-element.15) | copy-start | bytes 393220
  32.4 8.1 %copy-start.3 = (bf16[32,16,128]{2,1,0:T(8,128)(2,1)S(1)}, bf16[32,16,128]{2,1,0:T(8,128)(2,1)}, u32[]{:S(2)}) copy-start(bf16[32,16,128]{2,1,0:T(8,128)(2,1)} %get-tuple-element.17) | copy-start | bytes 393220
  40.7 8.0 %collective-permute-start.2 = (bf16[65,2304]{1,0:T(8,128)(2,1)S(1)}, bf16[65,2304]{1,0:T(8,128)(2,1)S(1)}, u32[]{:S(2)}, u32[]{:S(2)}) collective-permute-start(bf16[65,2304]{1,0:T(8,128)(2,1)S(1)} %maximum_maximum_fusion), channel_id=1, source_target_pairs={{0,1},{1,2},{2,3},{4,5},{5,6},{6,7},{8,9},{9,10},{10,11},{12,13},{... | collective-permute-start | bytes 898568 | tf_op jit(solution)/shard_map/ppermute | solution.py:325
  44.8 8.4 %collective-permute-start.3 = (bf16[65,2304]{1,0:T(8,128)(2,1)S(1)}, bf16[65,2304]{1,0:T(8,128)(2,1)S(1)}, u32[]{:S(2)}, u32[]{:S(2)}) collective-permute-start(bf16[65,2304]{1,0:T(8,128)(2,1)S(1)} %maximum_maximum_fusion.1), channel_id=1, source_target_pairs={{1,0},{2,1},{3,2},{5,4},{6,5},{7,6},{9,8},{10,9},{11,10},{13,12},{... | collective-permute-start | bytes 898568 | tf_op jit(solution)/shard_map/ppermute | solution.py:326

commit v3 on v2

--- a/solution.py
+++ b/solution.py
@@ -15,16 +15,23 @@
 WGROUP = 4
 
 
-def toeplitz(taps, channels):
-    kinds = taps.shape[0]
-    base = taps.reshape(kinds, 3, 3, 3, channels, channels).transpose(0, 3, 4, 1, 2, 5)
-    base = base.reshape(kinds, 3, channels, 3, 3 * channels)
-    rows = [
-        jnp.pad(base, ((0, 0),) * 4 + ((y * channels, (GROUP - 1 - y) * channels),))
-        for y in range(GROUP)
-    ]
-    full = jnp.stack(rows, axis=2)
-    return full.reshape(kinds, 3 * GROUP * channels, 3 * (GROUP + 2) * channels)
+def toeplitz(taps_ref, kind, opposite, dst, channels):
+    c = channels
+    span = (GROUP + 2) * c
+    for p in range(3):
+        for r in range(3):
+            base = None
+            for q in range(3):
+                tap = 9 * p + 3 * q + r
+                value = taps_ref[kind, 26 - tap if opposite else tap]
+                value = jnp.concatenate(
+                    [value, jnp.zeros((c, span - LANES), jnp.float32)], axis=1
+                )
+                base = value if base is None else base + pltpu.roll(value, q * c, 1)
+            for y in range(GROUP):
+                row = (r * GROUP + y) * c
+                moved = pltpu.roll(base, y * c, 1) if y else base
+                dst[row : row + c, p * span : (p + 1) * span] = moved.astype(jnp.bfloat16)
 
 
 def shifted(value, step):
@@ -63,11 +70,13 @@
 
 def grads_kernel(
     channels, ny, nx,
-    in_ref, cot_ref, mask_ref, xlo_ref, xhi_ref, ylo_ref, yhi_ref, w_ref, bias_ref,
+    in_ref, cot_ref, mask_ref, xlo_ref, xhi_ref, ylo_ref, yhi_ref, taps_ref, bias_ref,
     pre_ref, grad_ref,
-    s_in, s_cot, hid, hid_sh, pre_sh, acc1, acc2, bias_acc,
+    s_in, s_cot, hid, hid_sh, pre_sh, acc1, acc2, bias_acc, w_ref,
 ):
     c = channels
+    toeplitz(taps_ref, 0, False, w_ref.at[0], c)
+    toeplitz(taps_ref, 1, True, w_ref.at[1], c)
     rows = ny * c
     n = nx * LANES
     wide = n + 2 * LANES
@@ -156,9 +165,10 @@
 
 
 def input_kernel(
-    channels, ny, nx, pre_ref, sides_ref, ends_ref, mask_ref, w_ref, out_ref, pre
+    channels, ny, nx, pre_ref, sides_ref, ends_ref, mask_ref, taps_ref, out_ref, pre, w_ref
 ):
     c = channels
+    toeplitz(taps_ref, 2, True, w_ref, c)
     n = nx * LANES
     rows = ny * c
     pre[:c, :] = ends_ref[0]
@@ -172,7 +182,7 @@
         @pl.loop(0, nx // 2)
         def _(pair):
             col = pl.multiple_of(pair * 2 * LANES, 2 * LANES)
-            outs = conv_rows(w_ref[2], pre, y0 * c, col, c)
+            outs = conv_rows(w_ref[...], pre, y0 * c, col, c)
             for half in range(2):
                 keep = keep_rows(mask_ref, y0 + 1, col + (1 + half) * LANES, c)
                 out_ref[y0 * c : y0 * c + m6, pl.ds(col + half * LANES, LANES)] = (
@@ -350,13 +360,10 @@
     full_mask = full_mask.astype(jnp.float32).reshape(ny + 2, 1, (nx + 2) * nz)
 
     taps = jnp.stack(
-        [
-            conv_first,
-            conv_second[::-1].transpose(0, 2, 1),
-            conv_first[::-1].transpose(0, 2, 1),
-        ]
-    )
-    weights = toeplitz(taps, c)
+        [conv_first, conv_second.transpose(0, 2, 1), conv_first.transpose(0, 2, 1)]
+    ).astype(jnp.float32)
+    taps = jnp.pad(taps, ((0, 0), (0, 0), (0, 0), (0, LANES - c)))
+    matrix = (3 * GROUP * c, 3 * (GROUP + 2) * c)
     bias = jnp.broadcast_to(bias_first[None, :, None], (GROUP, c, LANES)).reshape(-1, LANES)
 
     wide, narrow = lax.axis_size("wide"), lax.axis_size("narrow")
@@ -385,10 +392,11 @@
             pltpu.VMEM(acc_shape, jnp.float32),
             pltpu.VMEM(acc_shape, jnp.float32),
             pltpu.VMEM((c, LANES), jnp.float32),
+            pltpu.VMEM((2,) + matrix, bf),
         ],
         compiler_params=params,
         name="local_grads",
-    )(own_in, own_cot, full_mask, xlo, xhi, ylo, yhi, weights, bias)
+    )(own_in, own_cot, full_mask, xlo, xhi, ylo, yhi, taps, bias)
 
     scale = 1.0 / math.sqrt(nx * wide * ny * narrow * nz)
     grads, sides, ends = total(grads, pre, c, wide, narrow, scale)
@@ -397,10 +405,10 @@
         out_shape=jax.ShapeDtypeStruct(shape, bf),
         in_specs=[vmem] * 5,
         out_specs=vmem,
-        scratch_shapes=[pltpu.VMEM(halo_shape, bf)],
+        scratch_shapes=[pltpu.VMEM(halo_shape, bf), pltpu.VMEM(matrix, bf)],
         compiler_params=params,
         name="input_grad",
-    )(pre, sides, ends, full_mask, weights)
+    )(pre, sides, ends, full_mask, taps)
     input_grad = out.reshape(ny, c, nx, nz).transpose(1, 2, 0, 3)
     both = grads[: 18 * c, : 3 * c].reshape(2, 3, 3, c, 3, c)
     first_grad = both[0].transpose(0, 3, 1, 2, 4).reshape(27, c, c)

time: 140 us -> 122 us (0.87)
  local copies, waits for them, and re-layouts: 39.7 us -> 18.9 us
  waiting for transfers between devices: 6.12 us -> 9.33 us
  other arithmetic: 3.64 us -> 1.35 us
  Pallas kernels: 77.3 us -> 79 us
    reshape x2 -> x0, local copies, waits for them, and re-layouts: 9.58 us -> none  [the longest x1 7.97 us: toeplitz(): return full.reshape(kinds, 3 * GROUP * channels, 3 * (GROUP + 2) * channels)]
    another operation x5 -> x0, local copies, waits for them, and re-layouts: 5.96 us -> none  [the longest x2 4.48 us: toeplitz(): full = jnp.stack(rows, axis=2)]
    ppermute x2, waiting for transfers between devices: 1.69 us -> 6.69 us  [exchange(): lo = lax.ppermute(tail, axis, [(i, i + 1) for i in range(count - 1)])]
    slice x5, local copies, waits for them, and re-layouts: 7.44 us -> 4.52 us  [rows(): own[r0:r1]]
    ppermute x2, waiting for transfers between devices: 4.43 us -> 2.64 us  [exchange(): hi = lax.ppermute(head, axis, [(i + 1, i) for i in range(count - 1)])]
    transpose x1 -> x0, other arithmetic: 1.75 us -> none  [toeplitz(): taps.reshape(kinds, 3, 3, 3, channels, channels).transpose(0, 3, 4, 1, 2, 5)]
    transpose x1, local copies, waits for them, and re-layouts: 2.13 us -> 0.54 us  [body(): own_cot = cotangent.transpose(2, 0, 1, 3).reshape(ny * c, nx * nz)]
    transpose x1, local copies, waits for them, and re-layouts: 0.54 us -> 2.13 us  [body(): own_in = inputs.transpose(2, 0, 1, 3).reshape(ny * c, nx * nz)]
  transfers between devices with their start and end apart: 4 -> 4, of which waited for: 2 -> 3; matrix products, arithmetic and copies ran while one was open for 19% -> 4% of each run, Pallas kernels for 0% -> 0%
where the time goes in v3:
time: 122 us; the launch traced here: 121 us
  Pallas kernels  79 us (65%)
  local copies, waits for them, and re-layouts  18.9 us (15%)
  starting transfers between devices  11.8 us (10%)
  waiting for transfers between devices  9.33 us (8%)
  other arithmetic  1.35 us (1%)
    pallas_call x1, Pallas kernels, body(): pl.pallas_call(functools.partial(grads_kernel, c, ny, nx), out_shape=(jax...  38.8 us
    pallas_call x1, Pallas kernels, total(): pl.pallas_call(functools.partial(total_kernel, wide, narrow, scale, chann...  26.1 us
    pallas_call x1, Pallas kernels, body(): pl.pallas_call(functools.partial(input_kernel, c, ny, nx), out_shape=jax....  14.1 us
    ppermute x2, starting transfers between devices, exchange(): lo = lax.ppermute(tail, axis, [(i, i + 1) for i in range(count - 1)])  7.96 us
    ppermute x2, waiting for transfers between devices, exchange(): lo = lax.ppermute(tail, axis, [(i, i + 1) for i in range(count - 1)])  6.69 us
    slice x5, local copies, waits for them, and re-layouts, rows(): own[r0:r1]  4.52 us
    ppermute x2, starting transfers between devices, exchange(): hi = lax.ppermute(head, axis, [(i + 1, i) for i in range(count - 1)])  3.82 us
    unnamed x20, local copies, waits for them, and re-layouts  3.78 us
  transfers between devices with their start and end apart: 4, of which 3 were waited for; matrix products, arithmetic and copies ran while one was open for 4% of the time, Pallas kernels for 0%

profile of v3, /device:TPU:1, one launch (start us, length us, event | category | flops | bytes accessed | tf_op | source)
XLA Modules:
  0.0 121.4 jit_solution(8935412852025023430)
XLA Ops:
  0.6 0.7 fusion.6
  1.7 2.1 %copy.37 = bf16[16,32,16,128]{3,2,1,0:T(8,128)(2,1)S(1)} copy(bf16[16,32,16,128]{3,0,2,1:T(8,128)(2,1)} %bitcast.69) | data formatting | bytes 4194304 | tf_op jit(solution)/shard_map/transpose | solution.py:330
  3.9 0.5 copy.63
  4.4 1.1 copy-done.3
  5.6 0.5 copy.38
  6.1 0.5 copy.62
  6.8 1.4 %collective-permute-start.1 = (bf16[1040,128]{1,0:T(8,128)(2,1)S(1)}, bf16[1040,128]{1,0:T(8,128)(2,1)S(1)}, u32[]{:S(2)}, u32[]{:S(2)}) collective-permute-start(bf16[1040,128]{1,0:T(8,128)(2,1)S(1)} %pad_maximum_fusion.1), channel_id=1, source_target_pairs={{4,0},{8,4},{12,8},{16,12},{20,16},{24,20},{28,24},{5,1},{9,5},{13... | collective-permute-start | bytes 798728 | tf_op jit(solution)/shard_map/ppermute | solution.py:336
  8.3 4.6 %collective-permute-start = (bf16[1040,128]{1,0:T(8,128)(2,1)S(1)}, bf16[1040,128]{1,0:T(8,128)(2,1)S(1)}, u32[]{:S(2)}, u32[]{:S(2)}) collective-permute-start(bf16[1040,128]{1,0:T(8,128)(2,1)S(1)} %pad_maximum_fusion), channel_id=1, source_target_pairs={{0,4},{4,8},{8,12},{12,16},{16,20},{20,24},{24,28},{1,5},{5,9},{9,... | collective-permute-start | bytes 798728 | tf_op jit(solution)/shard_map/ppermute | solution.py:335
  12.9 3.0 %slice_reduce_fusion.3 = (bf16[32,16,128]{2,1,0:T(8,128)(2,1)S(1)}, bf16[32,16,128]{2,1,0:T(8,128)(2,1)S(1)}) fusion(bf16[16,32,16,128]{3,0,2,1:T(8,128)(2,1)} %bitcast.70), kind=kLoop, calls=%fused_computation.17 | loop fusion | bytes 524288 | tf_op jit(solution)/shard_map/slice | solution.py:352
  15.9 1.4 %slice_reduce_fusion.2 = (bf16[32,16,128]{2,1,0:T(8,128)(2,1)S(1)}, bf16[32,16,128]{2,1,0:T(8,128)(2,1)S(1)}) fusion(bf16[16,32,16,128]{3,0,2,1:T(8,128)(2,1)S(1)} %bitcast.72), kind=kLoop, calls=%fused_computation.16 | loop fusion | bytes 524288 | tf_op jit(solution)/shard_map/slice | solution.py:352
  18.2 5.5 %collective-permute-done.xlo_ref = bf16[1040,128]{1,0:T(8,128)(2,1)S(1)} collective-permute-done((bf16[1040,128]{1,0:T(8,128)(2,1)S(1)}, bf16[1040,128]{1,0:T(8,128)(2,1)S(1)}, u32[]{:S(2)}, u32[]{:S(2)}) %collective-permute-start) | collective-permute-done | bytes 266272 | tf_op jit(solution)/shard_map/ppermute | solution.py:335
  23.9 2.4 %collective-permute-start.3 = (bf16[65,2304]{1,0:T(8,128)(2,1)S(1)}, bf16[65,2304]{1,0:T(8,128)(2,1)S(1)}, u32[]{:S(2)}, u32[]{:S(2)}) collective-permute-start(bf16[65,2304]{1,0:T(8,128)(2,1)S(1)} %maximum_maximum_fusion.1), channel_id=1, source_target_pairs={{1,0},{2,1},{3,2},{5,4},{6,5},{7,6},{9,8},{10,9},{11,10},{13,12},{... | collective-permute-start | bytes 898568 | tf_op jit(solution)/shard_map/ppermute | solution.py:336
  26.3 3.3 %collective-permute-start.2 = (bf16[65,2304]{1,0:T(8,128)(2,1)S(1)}, bf16[65,2304]{1,0:T(8,128)(2,1)S(1)}, u32[]{:S(2)}, u32[]{:S(2)}) collective-permute-start(bf16[65,2304]{1,0:T(8,128)(2,1)S(1)} %maximum_maximum_fusion), channel_id=1, source_target_pairs={{0,1},{1,2},{2,3},{4,5},{5,6},{6,7},{8,9},{9,10},{10,11},{12,13},{... | collective-permute-start | bytes 898568 | tf_op jit(solution)/shard_map/ppermute | solution.py:335
  29.7 2.6 %collective-permute-done.3.yhi_ref = bf16[65,2304]{1,0:T(8,128)(2,1)S(1)} collective-permute-done((bf16[65,2304]{1,0:T(8,128)(2,1)S(1)}, bf16[65,2304]{1,0:T(8,128)(2,1)S(1)}, u32[]{:S(2)}, u32[]{:S(2)}) %collective-permute-start.3) | collective-permute-done | bytes 299552 | tf_op jit(solution)/shard_map/ppermute | solution.py:336
  32.3 1.2 collective-permute-done.2.ylo_ref
  33.9 38.8 %local_grads.1 = (bf16[512,2048]{1,0:T(8,128)(2,1)S(1)}, f32[768,128]{1,0:T(8,128)S(1)}) custom-call(bf16[512,2048]{1,0:T(8,128)(2,1)} %bitcast.63, bf16[512,2048]{1,0:T(8,128)(2,1)} %bitcast.65, f32[18,1,2304]{2,1,0:T(1,128)S(1)} %maximum_convert_fusion.mask_ref, bf16[1040,128]{1,0:T(8,128)(2,1)S(1)} %collective-permute-done.xlo_ref, ...), custom_call_target="tpu_custom_call" | custom-call | tf_op jit(solution)/shard_map/local_grads/pallas_call | solution.py:378
  72.7 26.1 %total.1 = (f32[4,8,24,128]{3,2,1,0:T(8,128)S(1)}, bf16[2,512,128]{2,1,0:T(8,128)(2,1)S(1)}, bf16[2,32,2304]{2,1,0:T(8,128)(2,1)S(1)}) custom-call(f32[4,8,24,128]{3,2,1,0:T(8,128)S(1)} %bitcast.59, bf16[512,2048]{1,0:T(8,128)(2,1)S(1)} %get-tuple-element.9.pre_ref), custom_call_target="tpu_custom_call" | custom-call | tf_op jit(solution)/shard_map/total/pallas_call | solution.py:299
  98.9 14.1 %input_grad.1 = bf16[512,2048]{1,0:T(8,128)(2,1)S(1)} custom-call(bf16[512,2048]{1,0:T(8,128)(2,1)} %copy-done, bf16[2,512,128]{2,1,0:T(8,128)(2,1)S(1)} %get-tuple-element.11.sides_ref, bf16[2,32,2304]{2,1,0:T(8,128)(2,1)S(1)} %get-tuple-element.12.ends_ref, f32[18,1,2304]{2,1,0:T(1,128)S(1)} %maximum_convert_fusion.mask_ref, ...), custom_call_target="tpu_custom_call" | custom-call | tf_op jit(solution)/shard_map/input_grad/pallas_call | solution.py:403
  113.0 0.6 copy.54
  113.6 3.8 %copy.64 = bf16[16,32,16,128]{3,0,2,1:T(8,128)(2,1)} copy(bf16[16,32,16,128]{3,2,1,0:T(8,128)(2,1)S(1)} %bitcast.66) | data formatting | bytes 4194304 | tf_op jit(solution)/shard_map/reshape | solution.py:412
  117.4 0.6 copy.47
  118.2 1.1 rev.3
  119.4 1.0 copy.45
  120.6 0.8 copy.44
  (51 shorter events, 2.4 us)
Async XLA Ops:
  3.8 1.7 %copy-start.3 = (bf16[32,16,16,128]{3,2,1,0:T(8,128)(2,1)S(1)}, bf16[32,16,16,128]{3,2,1,0:T(8,128)(2,1)}, u32[]{:S(2)}) copy-start(bf16[32,16,16,128]{3,2,1,0:T(8,128)(2,1)} %param.7) | copy-start | bytes 6291460
  4.4 2.3 %copy-start.1 = (bf16[64,8,16,128]{3,1,2,0:T(8,128)(2,1)}, bf16[64,8,16,128]{3,1,2,0:T(8,128)(2,1)S(1)}, u32[]{:S(2)}) copy-start(bf16[64,8,16,128]{3,1,2,0:T(8,128)(2,1)S(1)} %copy.63) | copy-start | bytes 6291460
  6.6 10.7 %copy-start.2 = (bf16[64,8,16,128]{3,1,2,0:T(8,128)(2,1)}, bf16[64,8,16,128]{3,1,2,0:T(8,128)(2,1)S(1)}, u32[]{:S(2)}) copy-start(bf16[64,8,16,128]{3,1,2,0:T(8,128)(2,1)S(1)} %copy.62) | copy-start | bytes 6291460
  6.8 10.7 %copy-start.6 = (f32[32]{0:T(128)S(1)}, f32[32]{0:T(128)}, u32[]{:S(2)}) copy-start(f32[32]{0:T(128)} %param.11) | copy-start | bytes 388
  6.8 10.8 %copy-start.5 = (bf16[27,32,32]{2,1,0:T(8,128)(2,1)S(1)}, bf16[27,32,32]{2,1,0:T(8,128)(2,1)}, u32[]{:S(2)}) copy-start(bf16[27,32,32]{2,1,0:T(8,128)(2,1)} %param.10) | copy-start | bytes 165892
  6.8 11.0 %copy-start.4 = (bf16[27,32,32]{2,1,0:T(8,128)(2,1)S(1)}, bf16[27,32,32]{2,1,0:T(8,128)(2,1)}, u32[]{:S(2)}) copy-start(bf16[27,32,32]{2,1,0:T(8,128)(2,1)} %param.9) | copy-start | bytes 165892
  6.8 11.3 %collective-permute-start.1 = (bf16[1040,128]{1,0:T(8,128)(2,1)S(1)}, bf16[1040,128]{1,0:T(8,128)(2,1)S(1)}, u32[]{:S(2)}, u32[]{:S(2)}) collective-permute-start(bf16[1040,128]{1,0:T(8,128)(2,1)S(1)} %pad_maximum_fusion.1), channel_id=1, source_target_pairs={{4,0},{8,4},{12,8},{16,12},{20,16},{24,20},{28,24},{5,1},{9,5},{13... | collective-permute-start | bytes 798728 | tf_op jit(solution)/shard_map/ppermute | solution.py:336
  8.3 15.4 %collective-permute-start = (bf16[1040,128]{1,0:T(8,128)(2,1)S(1)}, bf16[1040,128]{1,0:T(8,128)(2,1)S(1)}, u32[]{:S(2)}, u32[]{:S(2)}) collective-permute-start(bf16[1040,128]{1,0:T(8,128)(2,1)S(1)} %pad_maximum_fusion), channel_id=1, source_target_pairs={{0,4},{4,8},{8,12},{12,16},{16,20},{20,24},{24,28},{1,5},{5,9},{9,... | collective-permute-start | bytes 798728 | tf_op jit(solution)/shard_map/ppermute | solution.py:335
  23.9 8.4 %collective-permute-start.3 = (bf16[65,2304]{1,0:T(8,128)(2,1)S(1)}, bf16[65,2304]{1,0:T(8,128)(2,1)S(1)}, u32[]{:S(2)}, u32[]{:S(2)}) collective-permute-start(bf16[65,2304]{1,0:T(8,128)(2,1)S(1)} %maximum_maximum_fusion.1), channel_id=1, source_target_pairs={{1,0},{2,1},{3,2},{5,4},{6,5},{7,6},{9,8},{10,9},{11,10},{13,12},{... | collective-permute-start | bytes 898568 | tf_op jit(solution)/shard_map/ppermute | solution.py:336
  26.3 7.2 %collective-permute-start.2 = (bf16[65,2304]{1,0:T(8,128)(2,1)S(1)}, bf16[65,2304]{1,0:T(8,128)(2,1)S(1)}, u32[]{:S(2)}, u32[]{:S(2)}) collective-permute-start(bf16[65,2304]{1,0:T(8,128)(2,1)S(1)} %maximum_maximum_fusion), channel_id=1, source_target_pairs={{0,1},{1,2},{2,3},{4,5},{5,6},{6,7},{8,9},{9,10},{10,11},{12,13},{... | collective-permute-start | bytes 898568 | tf_op jit(solution)/shard_map/ppermute | solution.py:335
  72.7 26.2 %copy-start = (bf16[512,2048]{1,0:T(8,128)(2,1)}, bf16[512,2048]{1,0:T(8,128)(2,1)S(1)}, u32[]{:S(2)}) copy-start(bf16[512,2048]{1,0:T(8,128)(2,1)S(1)} %get-tuple-element.9.pre_ref) | copy-start | bytes 6291460
